TPU v7x, 32 devices: a whole 2x2x4 slice. The times are simulated.
32 devices in a mesh: wide: 8 (over y, x, core), narrow: 4 (over z).
Axes of the slice: x: 2, y: 2, z: 4, core: 2. Of those that a mesh axis runs over, the one named last changes fastest.
Arguments:
- tile_flow_speed: float32 [512, 3, 4096], P(('wide', 'narrow')), may hold values from -3 to 3
- tile_stress_mean: float32 [512, 4096], P(('wide', 'narrow')), may hold values from -3 to 3
- tile_heat_state: float32 [512, 4096], P(('wide', 'narrow')), may hold values from 0 to 1
- tile_drag_coefficient: float32 [512, 4096], P(('wide', 'narrow')), may hold values from 0.5 to 2
- marker_attributes: float32 [8, 262144], P(None, ('wide', 'narrow')), may hold values from -6 to 6
- marker_holding_tile: int32 [262144], P(('wide', 'narrow')), may hold values from 0 to 511, as said below
- marker_voxel_number: int32 [262144], P(('wide', 'narrow')), may hold values from 0 to 4095
- prior_slot_of_tile: int32 [512], P(('wide', 'narrow')), may hold values from 0 to 511, as said below
Outputs:
- velocity: float32 [3, 128, 128, 128], P(None, 'wide', 'narrow')
- pressure: float32 [128, 128, 128], P('wide', 'narrow')
- heat_on_fresh_grid: float32 [128, 128, 128], P('wide', 'narrow')
- bin_mean_attributes: float32 [8, 32, 32, 32], P(None, 'wide', 'narrow')
Inputs may be any that keep to these rules, and one draw needn't show every extreme that they name: prior_slot_of_tile is a permutation: new owner q // 16 holds at place q % 16 the block that old owner prior_slot_of_tile[q] // 16 held at place prior_slot_of_tile[q] % 16. Every old owner sends to every new owner either none or exactly 1 of its blocks. `marker_holding_tile`: the tracer at position t is stored on old owner t // 8192 and lies in one of that owner's blocks. The tracers of one old owner whose blocks go to one new owner number at most 640, and every old owner has exactly 640 for one of its new owners.
All inputs are finite; a program needn't handle non-finite values.
Results may differ from a plain program's by a relative error of at most 0.00013.
Values sent between devices are 32-bit elements; how exact they have to be, the bound alone decides.
A program may use at most 256 MiB of HBM per device.

v0:
```python
import functools

import jax
import jax.numpy as jnp
from jax import lax
from jax.experimental import pallas as pl
from jax.experimental.pallas import tpu as pltpu
from jax.sharding import PartitionSpec as P

BS = 16
LX = 1
LY = 2
LZ = 8
SWEEPS = 3
BINS = 64

MIX_WEIGHTS = (0.3, -0.25, 0.2, -0.15, 0.35, -0.3, 0.25, -0.2)
RELAX_WEIGHT = 0.7
PRESSURE_WEIGHT = 0.3
HEAT_FACTOR = 2.0
DENSITY_FACTOR = 4.0
MESH = pl.DeviceIdType.MESH


def choose_kernel(
    mine_ref, block_ref, table, send_sems, recv_sems, *, wide_count, narrow_count, blocks
):
    count = wide_count * narrow_count
    me = lax.axis_index("wide") * narrow_count + lax.axis_index("narrow")

    def place(step):
        return lax.rem(me + step, count)

    def coordinates(step):
        other = place(step)
        return (lax.div(other, narrow_count), lax.rem(other, narrow_count))

    barrier = pltpu.get_barrier_semaphore()

    def greet(step, carry):
        pl.semaphore_signal(barrier, inc=1, device_id=coordinates(step), device_id_type=MESH)
        return carry

    lax.fori_loop(1, count, greet, 0)
    pl.semaphore_wait(barrier, count - 1)

    def copy_of(step, target):
        return pltpu.make_async_remote_copy(
            src_ref=mine_ref.at[0],
            dst_ref=table.at[target],
            send_sem=send_sems.at[step],
            recv_sem=recv_sems.at[step],
            device_id=coordinates(step),
            device_id_type=MESH,
        )

    def send(step, carry):
        copy_of(step, me).start()
        return carry

    lax.fori_loop(1, count, send, 0)
    table[me] = mine_ref[0]

    def finish(step, carry):
        copy_of(step, place(count - step)).wait_recv()
        copy_of(step, me).wait_send()
        return carry

    lax.fori_loop(1, count, finish, 0)
    local_old = table[...] - me * blocks
    is_mine = (local_old >= 0) & (local_old < blocks)
    block_ref[...] = jnp.sum(jnp.where(is_mine, local_old, 0), axis=2)


def choose_blocks(prior_slots):
    wide_count, narrow_count = lax.axis_size("wide"), lax.axis_size("narrow")
    count, blocks = wide_count * narrow_count, prior_slots.shape[0]
    padded = jnp.pad(prior_slots, (0, 128 - blocks), constant_values=-1).reshape(1, 1, 128)
    vmem = pl.BlockSpec(memory_space=pltpu.VMEM)
    return pl.pallas_call(
        functools.partial(
            choose_kernel, wide_count=wide_count, narrow_count=narrow_count, blocks=blocks
        ),
        out_shape=jax.ShapeDtypeStruct((count, 1), jnp.int32),
        in_specs=[vmem],
        out_specs=vmem,
        scratch_shapes=[
            pltpu.VMEM((count, 1, 128), jnp.int32),
            pltpu.SemaphoreType.DMA((count,)),
            pltpu.SemaphoreType.DMA((count,)),
        ],
        compiler_params=pltpu.CompilerParams(collective_id=2, has_side_effects=True),
    )(padded).reshape(count)


def exchange_kernel(
    send_ref, out_ref, landed, send_sems, recv_sems, *, wide_count, narrow_count
):
    count = wide_count * narrow_count
    me = lax.axis_index("wide") * narrow_count + lax.axis_index("narrow")

    def place(step):
        return lax.rem(me + step, count)

    def coordinates(step):
        other = place(step)
        return (lax.div(other, narrow_count), lax.rem(other, narrow_count))

    barrier = pltpu.get_barrier_semaphore()

    def greet(step, carry):
        pl.semaphore_signal(barrier, inc=1, device_id=coordinates(step), device_id_type=MESH)
        return carry

    lax.fori_loop(1, count, greet, 0)
    pl.semaphore_wait(barrier, count - 1)

    def copy_of(step, target):
        return pltpu.make_async_remote_copy(
            src_ref=send_ref.at[place(step)],
            dst_ref=landed.at[target],
            send_sem=send_sems.at[step],
            recv_sem=recv_sems.at[step],
            device_id=coordinates(step),
            device_id_type=MESH,
        )

    def send(step, carry):
        copy_of(step, me).start()
        return carry

    lax.fori_loop(1, count, send, 0)
    landed[me] = send_ref[me]

    def finish(step, carry):
        copy_of(step, place(count - step)).wait_recv()
        copy_of(step, me).wait_send()
        return carry

    lax.fori_loop(1, count, finish, 0)
    out_ref[...] = landed[...]


def exchange(entries):
    wide_count, narrow_count = lax.axis_size("wide"), lax.axis_size("narrow")
    count = wide_count * narrow_count
    vmem = pl.BlockSpec(memory_space=pltpu.VMEM)
    return pl.pallas_call(
        functools.partial(exchange_kernel, wide_count=wide_count, narrow_count=narrow_count),
        out_shape=jax.ShapeDtypeStruct(entries.shape, entries.dtype),
        in_specs=[vmem],
        out_specs=vmem,
        scratch_shapes=[
            pltpu.VMEM(entries.shape, entries.dtype),
            pltpu.SemaphoreType.DMA((count,)),
            pltpu.SemaphoreType.DMA((count,)),
        ],
        compiler_params=pltpu.CompilerParams(
            collective_id=3, has_side_effects=True, vmem_limit_bytes=32 * 1024 * 1024
        ),
    )(entries)


def bin_kernel(base_ref, holder_ref, voxel_ref, attr_ref, mean_ref, *, blocks, chunk):
    props, tracers = attr_ref.shape
    total_bins = blocks * BINS
    base = base_ref[0]
    bin_ids = lax.broadcasted_iota(jnp.int32, (total_bins, chunk), 0)

    def step(turn, sums):
        at = pl.ds(pl.multiple_of(turn * chunk, chunk), chunk)
        voxel = voxel_ref[:, at]
        key = (
            (holder_ref[:, at] - base) * BINS
            + (voxel >> 10) * 16
            + ((voxel >> 6) & 3) * 4
            + ((voxel >> 2) & 3)
        )
        table = jnp.where(bin_ids == key, 1.0, 0.0).astype(jnp.bfloat16)
        values = attr_ref[:, at]
        high = values.astype(jnp.bfloat16)
        rest = values - high.astype(jnp.float32)
        middle = rest.astype(jnp.bfloat16)
        low = (rest - middle.astype(jnp.float32)).astype(jnp.bfloat16)
        ones = jnp.ones((props, chunk), jnp.bfloat16)
        rows = jnp.concatenate([high, middle, low, ones], axis=0)
        return sums + lax.dot_general(
            rows, table, (((1,), (1,)), ((), ())), preferred_element_type=jnp.float32
        )

    sums = lax.fori_loop(
        0, tracers // chunk, step, jnp.zeros((4 * props, total_bins), jnp.float32)
    )
    total = sums[:props] + sums[props : 2 * props] + sums[2 * props : 3 * props]
    mean_ref[...] = total / jnp.maximum(sums[3 * props :], 1.0)


def bin_means(base, holder, voxel, attributes, blocks):
    props, tracers = attributes.shape
    chunk = 1024 if tracers % 1024 == 0 else tracers
    vmem = pl.BlockSpec(memory_space=pltpu.VMEM)
    return pl.pallas_call(
        functools.partial(bin_kernel, blocks=blocks, chunk=chunk),
        out_shape=jax.ShapeDtypeStruct((props, blocks * BINS), jnp.float32),
        in_specs=[pl.BlockSpec(memory_space=pltpu.SMEM), vmem, vmem, vmem],
        out_specs=vmem,
        compiler_params=pltpu.CompilerParams(vmem_limit_bytes=32 * 1024 * 1024),
        cost_estimate=pl.CostEstimate(
            flops=2 * 32 * tracers * blocks * BINS, bytes_accessed=40 * tracers, transcendentals=0
        ),
    )(base.reshape(1), holder.reshape(1, tracers), voxel.reshape(1, tracers), attributes)


def swap_groups(x):
    row = lax.broadcasted_iota(jnp.int32, x.shape, 1)
    group = lax.broadcasted_iota(jnp.int32, x.shape, 2) // BS
    for bit in (1, 2, 4):
        row_set = (row & bit) != 0
        group_set = (group & bit) != 0
        from_above = pltpu.roll(pltpu.roll(x, 8 - bit, 1), BS * bit, 2)
        from_below = pltpu.roll(pltpu.roll(x, bit, 1), 8 * BS - BS * bit, 2)
        x = jnp.where(
            row_set == group_set, x, jnp.where(group_set, from_above, from_below)
        )
    return x


def pick_kernel(index_ref, from_ref, to_ref, sems):
    count = to_ref.shape[0]

    def copy_of(i):
        return pltpu.make_async_copy(from_ref.at[index_ref[i]], to_ref.at[i], sems.at[i])

    for i in range(count):
        copy_of(i).start()
    for i in range(count):
        copy_of(i).wait()


def pick(index, array):
    return pl.pallas_call(
        pick_kernel,
        out_shape=jax.ShapeDtypeStruct(index.shape + array.shape[1:], array.dtype),
        in_specs=[
            pl.BlockSpec(memory_space=pltpu.SMEM),
            pl.BlockSpec(memory_space=pltpu.VMEM),
        ],
        out_specs=pl.BlockSpec(memory_space=pl.ANY),
        scratch_shapes=[pltpu.SemaphoreType.DMA(index.shape)],
        compiler_params=pltpu.CompilerParams(vmem_limit_bytes=32 * 1024 * 1024),
    )(index, array)


def unpack_kernel(slot_ref, recv_ref, mix_ref, state_ref, heat_ref, held, sems):
    places = LY * LZ
    copies = []
    for r in range(places):
        copies.append(
            pltpu.make_async_copy(
                recv_ref.at[slot_ref[r]], held.at[r // LZ, :, r % LZ, :], sems.at[r]
            )
        )
        copies[-1].start()
    for copy in copies:
        copy.wait()
    spread = (
        lax.broadcasted_iota(jnp.int32, (32, 128), 0)
        == lax.broadcasted_iota(jnp.int32, (32, 128), 1) // 4
    ).astype(jnp.float32)
    wide_mix = jnp.dot(
        mix_ref[...], spread, precision=lax.Precision.HIGHEST, preferred_element_type=jnp.float32
    )
    for y in range(LY):
        rows = slice(y * BS, (y + 1) * BS)
        for field in range(4):
            part = swap_groups(held[y, field * 32 : (field + 1) * 32])
            state_ref[field, :, rows, :] = part.reshape(BS, BS, 128)
        heat = swap_groups(held[y, 128:160]).reshape(BS, BS, 128)
        heat_ref[:, rows, :] = heat
        drag = swap_groups(held[y, 160:192]).reshape(BS, BS, 128)
        for layer in range(4):
            piece = wide_mix[layer * 8 + y * 4 : layer * 8 + y * 4 + 4]
            piece = jnp.concatenate(
                [jnp.broadcast_to(piece[j : j + 1], (4, 128)) for j in range(4)], axis=0
            )
            at = slice(layer * 4, layer * 4 + 4)
            state_ref[4, at, rows, :] = drag[at] * jnp.exp(
                HEAT_FACTOR * (0.5 - heat[at]) + piece[None]
            )


def unpack(slots, received, mixture):
    grid_shape = (BS, LY * BS, LZ * BS)
    vmem = pl.BlockSpec(memory_space=pltpu.VMEM)
    return pl.pallas_call(
        unpack_kernel,
        out_shape=(
            jax.ShapeDtypeStruct((5,) + grid_shape, jnp.float32),
            jax.ShapeDtypeStruct(grid_shape, jnp.float32),
        ),
        in_specs=[
            pl.BlockSpec(memory_space=pltpu.SMEM),
            pl.BlockSpec(memory_space=pl.ANY),
            vmem,
        ],
        out_specs=(vmem, vmem),
        scratch_shapes=[
            pltpu.VMEM((LY, 192, LZ, 128), jnp.float32),
            pltpu.SemaphoreType.DMA((LY * LZ,)),
        ],
        compiler_params=pltpu.CompilerParams(vmem_limit_bytes=32 * 1024 * 1024),
    )(slots, received, mixture)


def sweep_kernel(
    state_ref, heat_ref, velocity_ref, pressure_ref,
    pad_0, pad_1, pad_2, edge_out, edge_in, send_sems, recv_sems,
    *, wide_count, narrow_count,
):
    wide, narrow = lax.axis_index("wide"), lax.axis_index("narrow")
    nx, ny, nz = heat_ref.shape
    exists = (wide > 0, wide < wide_count - 1, narrow > 0, narrow < narrow_count - 1)
    partner = ((wide - 1, narrow), (wide + 1, narrow), (wide, narrow - 1), (wide, narrow + 1))
    barrier = pltpu.get_barrier_semaphore()
    pads = (pad_0, pad_1, pad_2)
    for pad in pads:
        fields = pad.shape[0]
        for x in (0, nx + 1):
            pad[:, x] = jnp.zeros((fields, ny, nz), jnp.float32)
    edge_in[...] = jnp.zeros(edge_in.shape, jnp.float32)
    for side in range(4):

        @pl.when(exists[side])
        def _(side=side):
            pl.semaphore_signal(barrier, inc=1, device_id=partner[side], device_id_type=MESH)

    pad_0[:, 1 : nx + 1] = state_ref[...]
    pl.semaphore_wait(barrier, sum(there.astype(jnp.int32) for there in exists))

    row = lax.broadcasted_iota(jnp.int32, (ny, nz), 0)
    column = lax.broadcasted_iota(jnp.int32, (ny, nz), 1)

    def copy_of(turn, side):
        pad = pads[turn]
        fields = pad.shape[0]
        if side == 0:
            source, target = pad.at[:, 1], pad.at[:, nx + 1]
        elif side == 1:
            source, target = pad.at[:, nx], pad.at[:, 0]
        else:
            source = edge_out.at[turn, side - 2, pl.ds(0, fields)]
            target = edge_in.at[turn, 3 - side, pl.ds(0, fields)]
        return pltpu.make_async_remote_copy(
            src_ref=source,
            dst_ref=target,
            send_sem=send_sems.at[turn, side],
            recv_sem=recv_sems.at[turn, side ^ 1],
            device_id=partner[side],
            device_id_type=MESH,
        )

    def arrival_of(turn, side):
        pad = pads[turn]
        fields = pad.shape[0]
        if side < 2:
            target = pad.at[:, 0 if side == 0 else nx + 1]
        else:
            target = edge_in.at[turn, side - 2, pl.ds(0, fields)]
        return pltpu.make_async_remote_copy(
            src_ref=target,
            dst_ref=target,
            send_sem=send_sems.at[turn, side],
            recv_sem=recv_sems.at[turn, side],
            device_id=partner[side],
            device_id_type=MESH,
        )

    for turn in range(SWEEPS):
        pad = pads[turn]
        for side in range(2):

            @pl.when(exists[side])
            def _(side=side):
                copy_of(turn, side).start()

        for field in range(pad.shape[0]):
            edge_out[turn, 0, field] = pad[field, 1 : nx + 1, 0, :]
            edge_out[turn, 1, field] = pad[field, 1 : nx + 1, ny - 1, :]
        for side in range(2, 4):

            @pl.when(exists[side])
            def _(side=side):
                copy_of(turn, side).start()

        for side in range(4):

            @pl.when(exists[side])
            def _(side=side):
                arrival_of(turn, side).wait_recv()

        def slab(x, carry, turn=turn, pad=pad):
            def around(ref, edges, field):
                centre = ref[field, x + 1]
                low = edges[0, field, pl.ds(x, 1), :]
                high = edges[1, field, pl.ds(x, 1), :]
                return (
                    centre,
                    ref[field, x + 2],
                    ref[field, x],
                    jnp.where(row == ny - 1, high, pltpu.roll(centre, ny - 1, 0)),
                    jnp.where(row == 0, low, pltpu.roll(centre, 1, 0)),
                    jnp.where(column == nz - 1, 0.0, pltpu.roll(centre, nz - 1, 1)),
                    jnp.where(column == 0, 0.0, pltpu.roll(centre, 1, 1)),
                )

            eta = around(pad_0, edge_in.at[0], 4)
            face = [0.5 * (eta[0] + eta[m]) for m in range(1, 7)]
            diagonal = face[0]
            for m in range(1, 6):
                diagonal = diagonal + face[m]
            scale = RELAX_WEIGHT / diagonal
            press = around(pad, edge_in.at[turn], 3)
            divergence = None
            for component in range(3):
                speed = around(pad, edge_in.at[turn], component)
                residual = face[0] * (speed[1] - speed[0])
                for m in range(1, 6):
                    residual = residual + face[m] * (speed[m + 1] - speed[0])
                up, down = 2 * component + 1, 2 * component + 2
                residual = residual - 0.5 * (press[up] - press[down])
                if component == 2:
                    residual = residual + DENSITY_FACTOR * heat_ref[x]
                moved = speed[0] + residual * scale
                if turn < SWEEPS - 1:
                    pads[turn + 1][component, x + 1] = moved
                else:
                    velocity_ref[component, x] = moved
                flux = 0.5 * (speed[up] - speed[down])
                divergence = flux if divergence is None else divergence + flux
            moved = press[0] - PRESSURE_WEIGHT * eta[0] * divergence
            if turn < SWEEPS - 1:
                pads[turn + 1][3, x + 1] = moved
            else:
                pressure_ref[x] = moved
            return carry

        lax.fori_loop(0, nx, slab, 0)

    for turn in range(SWEEPS):
        for side in range(4):

            @pl.when(exists[side])
            def _(turn=turn, side=side):
                copy_of(turn, side).wait_send()


def sweeps(state, heat):
    nx, ny, nz = heat.shape
    vmem = pl.BlockSpec(memory_space=pltpu.VMEM)
    return pl.pallas_call(
        functools.partial(
            sweep_kernel,
            wide_count=lax.axis_size("wide"),
            narrow_count=lax.axis_size("narrow"),
        ),
        out_shape=(
            jax.ShapeDtypeStruct((3, nx, ny, nz), jnp.float32),
            jax.ShapeDtypeStruct((nx, ny, nz), jnp.float32),
        ),
        in_specs=[vmem, vmem],
        out_specs=(vmem, vmem),
        scratch_shapes=[
            pltpu.VMEM((5, nx + 2, ny, nz), jnp.float32),
            pltpu.VMEM((4, nx + 2, ny, nz), jnp.float32),
            pltpu.VMEM((4, nx + 2, ny, nz), jnp.float32),
            pltpu.VMEM((SWEEPS, 2, 5, nx, nz), jnp.float32),
            pltpu.VMEM((SWEEPS, 2, 5, nx, nz), jnp.float32),
            pltpu.SemaphoreType.DMA((SWEEPS, 4)),
            pltpu.SemaphoreType.DMA((SWEEPS, 4)),
        ],
        compiler_params=pltpu.CompilerParams(
            collective_id=1, has_side_effects=True, vmem_limit_bytes=32 * 1024 * 1024
        ),
    )(state, heat)


def per_device(
    tile_flow_speed,
    tile_stress_mean,
    tile_heat_state,
    tile_drag_coefficient,
    marker_attributes,
    marker_holding_tile,
    marker_voxel_number,
    prior_slot_of_tile,
):
    wide_count = lax.axis_size("wide")
    narrow_count = lax.axis_size("narrow")
    my_index = lax.axis_index("wide") * narrow_count + lax.axis_index("narrow")
    blocks = prior_slot_of_tile.shape[0]
    props = marker_attributes.shape[0]
    block_for = choose_blocks(prior_slot_of_tile)
    stacked = jnp.concatenate(
        [
            tile_flow_speed.reshape(blocks, 96, 128),
            tile_stress_mean.reshape(blocks, 32, 128),
            tile_heat_state.reshape(blocks, 32, 128),
            tile_drag_coefficient.reshape(blocks, 32, 128),
        ],
        axis=1,
    )
    outgoing = pick(block_for, stacked)
    outgoing, marker_attributes = lax.optimization_barrier((outgoing, marker_attributes))
    received = lax.all_to_all(
        outgoing, ("wide", "narrow"), split_axis=0, concat_axis=0, tiled=True
    )
    means = bin_means(
        my_index * blocks, marker_holding_tile, marker_voxel_number, marker_attributes, blocks
    )
    by_block = means.reshape(props, blocks, BINS).transpose(1, 0, 2).reshape(blocks, 4, 128)
    received_means = exchange(pick(block_for, by_block))
    source_dev = prior_slot_of_tile // blocks
    arrived = pick(source_dev, received_means).reshape(LX, LY, LZ, props, 4, 4, 4)
    bin_mean_attributes = arrived.transpose(3, 0, 4, 1, 5, 2, 6)
    bin_mean_attributes = bin_mean_attributes.reshape(props, LX * 4, LY * 4, LZ * 4)
    mixture = MIX_WEIGHTS[0] * bin_mean_attributes[0]
    for index_p in range(1, props):
        mixture = mixture + MIX_WEIGHTS[index_p] * bin_mean_attributes[index_p]
    state, heat = unpack(source_dev, received, mixture.reshape(LY * BS, LZ * 4))
    velocity, pressure = sweeps(state, heat)
    return (velocity, pressure, heat, bin_mean_attributes)


def solution(mesh):
    in_specs = (
        P(("wide", "narrow"), None, None),
        P(("wide", "narrow"), None),
        P(("wide", "narrow"), None),
        P(("wide", "narrow"), None),
        P(None, ("wide", "narrow")),
        P(("wide", "narrow")),
        P(("wide", "narrow")),
        P(("wide", "narrow")),
    )
    out_specs = (
        P(None, "wide", "narrow", None),
        P("wide", "narrow", None),
        P("wide", "narrow", None),
        P(None, "wide", "narrow", None),
    )
    return jax.shard_map(
        per_device, mesh=mesh, in_specs=in_specs, out_specs=out_specs, check_vma=False
    )
```

profile of v0, /device:TPU:1, one launch (start us, length us, event | category | flops | bytes accessed | tf_op | source)
XLA Modules:
  0.0 137.3 jit_solution(13364740277805493286)
XLA Ops:
  0.6 1.2 pad_bitcast_fusion.mine_ref
  1.9 10.7 %shard_map.111 = s32[32,1]{1,0:T(8,128)} custom-call(s32[1,1,128]{2,1,0:T(1,128)} %pad_bitcast_fusion.mine_ref), custom_call_target="tpu_custom_call" | custom-call | tf_op jit(solution)/shard_map/pallas_call | solution.py:80
  12.6 1.0 copy.23
  13.6 1.0 copy.22
  14.6 1.0 copy.21
  15.6 0.5 copy.15
  16.2 0.6 reshape.93
  16.8 0.1 reduce.index_ref
  16.9 0.1 pad_maximum_fusion.from_ref
  17.0 5.1 %shard_map.112 = f32[32,192,128]{2,1,0:T(8,128)S(1)} custom-call(s32[32]{0:T(128)S(1)} %reduce.index_ref, f32[16,192,128]{2,1,0:T(8,128)S(1)} %pad_maximum_fusion.from_ref), custom_call_target="tpu_custom_call" | custom-call | tf_op jit(solution)/shard_map/pallas_call | solution.py:241
  22.1 1.6 %copy-done = f32[32,192,128]{2,1,0:T(8,128)} copy-done((f32[32,192,128]{2,1,0:T(8,128)}, f32[32,192,128]{2,1,0:T(8,128)S(1)}, u32[]{:S(2)}) %copy-start) | copy-done | bytes 3145752
  23.7 5.6 %all-to-all-start = ((f32[32,192,128]{2,1,0:T(8,128)}), f32[32,192,128]{2,1,0:T(8,128)S(1)}, u32[]{:S(2)}, u32[]{:S(2)}) async-start(f32[32,192,128]{2,1,0:T(8,128)} %copy-done), calls=%async_computation | async-start | bytes 6291456 | tf_op jit(solution)/shard_map/all_to_all | solution.py:514
  29.4 0.0 copy-start.7
  29.4 5.9 %shard_map.113 = f32[8,1024]{1,0:T(8,128)S(1)} custom-call(s32[1]{0:T(128)} %bitcast.1.base_ref, s32[1,8192]{1,0:T(1,128)S(1)} %bitcast.20, s32[1,8192]{1,0:T(1,128)S(1)} %bitcast.21, f32[8,8192]{1,0:T(8,128)S(1)} %copy-done.2), custom_call_target="tpu_custom_call" | custom-call | flops 536870912 | bytes 327680 | tf_op jit(solution)/shard_map/pallas_call | solution.py:202
  35.3 0.1 reshape.100
  35.5 0.1 reshape.101.from_ref
  35.5 1.0 shard_map.114.send_ref
  36.6 68.1 %shard_map.115.from_ref = f32[32,4,128]{2,1,0:T(4,128)S(1)} custom-call(f32[32,4,128]{2,1,0:T(4,128)S(1)} %shard_map.114.send_ref), custom_call_target="tpu_custom_call" | custom-call | tf_op jit(solution)/shard_map/pallas_call | solution.py:148
  104.8 0.8 shard_map.116
  105.6 0.1 copy.17
  105.7 1.1 reshape.102
  106.8 2.1 %copy.19 = f32[8,1,4,2,4,8,4]{0,6,5,4,3,2,1:T(4,128)} copy(f32[8,1,4,2,4,8,4]{5,3,6,4,2,0,1:T(2,128)} %bitcast.22) | data formatting | bytes 65536 | tf_op jit(solution)/shard_map/transpose | solution.py:524
  109.0 1.3 fusion
  110.2 0.3 copy.18
  110.5 0.1 reshape.107.mix_ref
  110.6 1.9 %copy.20 = f32[8,4,8,32]{3,2,1,0:T(8,128)} copy(f32[8,4,8,32]{0,3,2,1:T(8,128)} %bitcast.24) | data formatting | bytes 65536
  112.5 5.4 %shard_map.117 = (f32[5,16,32,128]{3,2,1,0:T(8,128)S(1)}, f32[16,32,128]{2,1,0:T(8,128)}) custom-call(s32[16]{0:T(128)S(1)} %and_select_fusion.index_ref.slot_ref, f32[32,192,128]{2,1,0:T(8,128)S(1)} %all-to-all-done.recv_ref, f32[32,32]{1,0:T(8,128)S(1)} %reshape.107.mix_ref), custom_call_target="tpu_custom_call" | custom-call | tf_op jit(solution)/shard_map/pallas_call | solution.py:295
  117.9 0.0 copy-start.1
  117.9 0.9 copy-done.1
  118.8 16.8 %shard_map.118 = (f32[3,16,32,128]{3,2,1,0:T(8,128)S(1)}, f32[16,32,128]{2,1,0:T(8,128)S(1)}) custom-call(f32[5,16,32,128]{3,2,1,0:T(8,128)S(1)} %get-tuple-element.12.state_ref, f32[16,32,128]{2,1,0:T(8,128)S(1)} %copy-done.1), custom_call_target="tpu_custom_call" | custom-call | tf_op jit(solution)/shard_map/pallas_call | solution.py:460
  135.7 0.9 copy.28
  136.6 0.7 copy.29
  (15 shorter events, 0.1 us)
Async XLA Ops:
  0.6 15.0 %copy-start.5 = (f32[16,3,4096]{2,0,1:T(8,128)S(1)}, f32[16,3,4096]{2,0,1:T(8,128)}, u32[]{:S(2)}) copy-start(f32[16,3,4096]{2,0,1:T(8,128)} %param.8) | copy-start | bytes 2359300
  15.6 1.2 copy-start.6
  22.1 1.6 %copy-start = (f32[32,192,128]{2,1,0:T(8,128)}, f32[32,192,128]{2,1,0:T(8,128)S(1)}, u32[]{:S(2)}) copy-start(f32[32,192,128]{2,1,0:T(8,128)S(1)} %shard_map.112) | copy-start | bytes 9437188
  23.7 5.7 %copy-start.2 = (f32[8,8192]{1,0:T(8,128)S(1)}, f32[8,8192]{1,0:T(8,128)}, u32[]{:S(2)}) copy-start(f32[8,8192]{1,0:T(8,128)} %attr_ref) | copy-start | bytes 786436
  23.7 5.7 %copy-start.3 = (s32[8192]{0:T(1024)S(1)}, s32[8192]{0:T(1024)}, u32[]{:S(2)}) copy-start(s32[8192]{0:T(1024)} %param.13) | copy-start | bytes 98308
  23.7 5.7 %copy-start.4 = (s32[8192]{0:T(1024)S(1)}, s32[8192]{0:T(1024)}, u32[]{:S(2)}) copy-start(s32[8192]{0:T(1024)} %param.14) | copy-start | bytes 98308
  23.7 88.8 %all-to-all-start = ((f32[32,192,128]{2,1,0:T(8,128)}), f32[32,192,128]{2,1,0:T(8,128)S(1)}, u32[]{:S(2)}, u32[]{:S(2)}) async-start(f32[32,192,128]{2,1,0:T(8,128)} %copy-done), calls=%async_computation | async-start | bytes 6291456 | tf_op jit(solution)/shard_map/all_to_all | solution.py:514
  29.4 75.4 %copy-start.7 = (s32[16]{0:T(128)S(1)}, s32[16]{0:T(128)}, u32[]{:S(2)}) copy-start(s32[16]{0:T(128)} %param.15) | copy-start | bytes 196
  117.9 1.0 copy-start.1
where the time goes:
time: 138 us; the launch traced here: 137 us
  Pallas kernels  114 us (83%)
  local copies, waits for them, and re-layouts  15.4 us (11%)
  starting transfers between devices  5.62 us (4%)
  other arithmetic  1.49 us (1%)
    pallas_call x1, Pallas kernels, exchange(): pl.pallas_call(functools.partial(exchange_kernel, wide_count=wide_count,...  68.1 us
    pallas_call x1, Pallas kernels, sweeps(): pl.pallas_call(functools.partial(sweep_kernel, wide_count=lax.axis_size('...  16.8 us
    pallas_call x1, Pallas kernels, choose_blocks(): pl.pallas_call(functools.partial(choose_kernel, wide_count=wide_count, na...  10.7 us
    unnamed x23, local copies, waits for them, and re-layouts  9.63 us
    pallas_call x3, Pallas kernels, pick(): pl.pallas_call(pick_kernel, out_shape=jax.ShapeDtypeStruct(index.shape +...  6.9 us
    pallas_call x1, Pallas kernels, bin_means(): pl.pallas_call(functools.partial(bin_kernel, blocks=blocks, chunk=chunk),...  5.93 us
    all_to_all x1, starting transfers between devices, per_device(): lax.all_to_all(outgoing, ('wide', 'narrow'), split_axis=0, concat_axis=0,...  5.62 us
    pallas_call x1, Pallas kernels, unpack(): pl.pallas_call(unpack_kernel, out_shape=(jax.ShapeDtypeStruct((5,) + grid...  5.39 us
  transfers between devices with their start and end apart: 1, of which 0 were waited for; matrix products, arithmetic and copies ran while one was open for 5% of the time, Pallas kernels for 55%

commit v1 on v0

v1 whole, which is shorter than its diff:
```python
import functools

import jax
import jax.numpy as jnp
from jax import lax
from jax.experimental import pallas as pl
from jax.experimental.pallas import tpu as pltpu
from jax.sharding import PartitionSpec as P

BS = 16
LX = 1
LY = 2
LZ = 8
SWEEPS = 3
BINS = 64
FIELDS = 6
AHEAD = 3

MIX_WEIGHTS = (0.3, -0.25, 0.2, -0.15, 0.35, -0.3, 0.25, -0.2)
RELAX_WEIGHT = 0.7
PRESSURE_WEIGHT = 0.3
HEAT_FACTOR = 2.0
DENSITY_FACTOR = 4.0
MESH = pl.DeviceIdType.MESH


def swap_groups(x):
    row = lax.broadcasted_iota(jnp.int32, x.shape, 1)
    group = lax.broadcasted_iota(jnp.int32, x.shape, 2) // BS
    for bit in (1, 2, 4):
        row_set = (row & bit) != 0
        group_set = (group & bit) != 0
        from_above = pltpu.roll(pltpu.roll(x, 8 - bit, 1), BS * bit, 2)
        from_below = pltpu.roll(pltpu.roll(x, bit, 1), 8 * BS - BS * bit, 2)
        x = jnp.where(
            row_set == group_set, x, jnp.where(group_set, from_above, from_below)
        )
    return x


def bin_sums(base, holder_ref, voxel_ref, attr_ref, blocks, chunk):
    props, tracers = attr_ref.shape
    total_bins = blocks * BINS
    bin_ids = lax.broadcasted_iota(jnp.int32, (total_bins, chunk), 0)

    def step(turn, sums):
        at = pl.ds(pl.multiple_of(turn * chunk, chunk), chunk)
        voxel = voxel_ref[:, at]
        key = (
            (holder_ref[:, at] - base) * BINS
            + (voxel >> 10) * 16
            + ((voxel >> 6) & 3) * 4
            + ((voxel >> 2) & 3)
        )
        table = jnp.where(bin_ids == key, 1.0, 0.0).astype(jnp.bfloat16)
        values = attr_ref[:, at]
        high = values.astype(jnp.bfloat16)
        rest = values - high.astype(jnp.float32)
        middle = rest.astype(jnp.bfloat16)
        low = (rest - middle.astype(jnp.float32)).astype(jnp.bfloat16)
        ones = jnp.ones((props, chunk), jnp.bfloat16)
        rows = jnp.concatenate([high, middle, low, ones], axis=0)
        return sums + lax.dot_general(
            rows, table, (((1,), (1,)), ((), ())), preferred_element_type=jnp.float32
        )

    sums = lax.fori_loop(
        0, tracers // chunk, step, jnp.zeros((4 * props, total_bins), jnp.float32)
    )
    total = sums[:props] + sums[props : 2 * props] + sums[2 * props : 3 * props]
    return total / jnp.maximum(sums[3 * props :], 1.0)


def relax_slab(x, eta_pad, eta_edges, pad, edges, heat_ref):
    ny, nz = heat_ref.shape[1:]
    row = lax.broadcasted_iota(jnp.int32, (ny, nz), 0)
    column = lax.broadcasted_iota(jnp.int32, (ny, nz), 1)

    def around(here, lower, upper, low, high):
        return (
            here,
            upper,
            lower,
            jnp.where(row == ny - 1, high, pltpu.roll(here, ny - 1, 0)),
            jnp.where(row == 0, low, pltpu.roll(here, 1, 0)),
            jnp.where(column == nz - 1, 0.0, pltpu.roll(here, nz - 1, 1)),
            jnp.where(column == 0, 0.0, pltpu.roll(here, 1, 1)),
        )

    def field(k):
        return around(
            pad[k, x + 1], pad[k, x], pad[k, x + 2],
            edges[0, k, pl.ds(x, 1), :], edges[1, k, pl.ds(x, 1), :],
        )

    eta = around(
        eta_pad[x + 1], eta_pad[x], eta_pad[x + 2],
        eta_edges[0, pl.ds(x, 1), :], eta_edges[1, pl.ds(x, 1), :],
    )
    face = [0.5 * (eta[0] + eta[m]) for m in range(1, 7)]
    diagonal = face[0]
    for m in range(1, 6):
        diagonal = diagonal + face[m]
    scale = RELAX_WEIGHT / diagonal
    press = field(3)
    divergence = None
    moved = []
    for component in range(3):
        speed = field(component)
        residual = face[0] * (speed[1] - speed[0])
        for m in range(1, 6):
            residual = residual + face[m] * (speed[m + 1] - speed[0])
        up, down = 2 * component + 1, 2 * component + 2
        residual = residual - 0.5 * (press[up] - press[down])
        if component == 2:
            residual = residual + DENSITY_FACTOR * heat_ref[x]
        moved.append(speed[0] + residual * scale)
        flux = 0.5 * (speed[up] - speed[down])
        divergence = flux if divergence is None else divergence + flux
    moved.append(press[0] - PRESSURE_WEIGHT * eta[0] * divergence)
    return moved


def migrate_kernel(
    row_ref, slot_ref, flow_ref, stress_ref, warm_ref, drag_ref, attr_ref, holder_ref, voxel_ref,
    pad_ref, edge_ref, eta_ref, eta_edge_ref, heat_ref, mean_ref,
    table, wanted, wanted_smem, raw, lined, mine, stage_0, stage_1, stage_2, stage_3, stage_4, stage_5,
    land_0, land_1, land_2, land_3, land_4, land_5,
    attr, holder, voxel, mean_mine, mean_stage, mean_land, mean_held, held, drag_grid,
    pad_0, pad_1, edge_0, edge_1, edge_out, eta_out,
    raw_sems, table_sems, data_send, data_recv, mean_sems,
    eta_send, eta_recv, halo_send, halo_recv, small_sem,
    *, wide_count, narrow_count,
):
    count = wide_count * narrow_count
    wide, narrow = lax.axis_index("wide"), lax.axis_index("narrow")
    me = wide * narrow_count + narrow
    blocks = raw.shape[1]
    nx, ny, nz = heat_ref.shape
    stages = (stage_0, stage_1, stage_2, stage_3, stage_4, stage_5)
    lands = (land_0, land_1, land_2, land_3, land_4, land_5)
    pads = (pad_0, pad_1, pad_ref)
    edges = (edge_0, edge_1, edge_ref)

    sources = (
        warm_ref, drag_ref, flow_ref.at[0], flow_ref.at[1], flow_ref.at[2], stress_ref,
    )
    loads = [
        pltpu.make_async_copy(source, raw.at[f], raw_sems.at[f]) for f, source in enumerate(sources)
    ]
    loads.append(pltpu.make_async_copy(attr_ref, attr, raw_sems.at[FIELDS]))
    loads.append(pltpu.make_async_copy(holder_ref, holder, raw_sems.at[FIELDS + 1]))
    loads.append(pltpu.make_async_copy(voxel_ref, voxel, raw_sems.at[FIELDS + 2]))
    for load in loads:
        load.start()

    for pad in pads:
        for x in (0, nx + 1):
            pad[:, x] = jnp.zeros((4, ny, nz), jnp.float32)
    for x in (0, nx + 1):
        eta_ref[x] = jnp.zeros((ny, nz), jnp.float32)
    for edge in edges:
        edge[...] = jnp.zeros(edge.shape, jnp.float32)
    eta_edge_ref[...] = jnp.zeros(eta_edge_ref.shape, jnp.float32)

    def others(act):
        near = [lax.rem(narrow + b, narrow_count) for b in range(narrow_count)]
        for b in range(1, narrow_count):
            act(wide, near[b])

        def row(a, carry):
            far = lax.rem(wide + a, wide_count)
            for b in range(narrow_count):
                act(far, near[b])
            return carry

        lax.fori_loop(1, wide_count, row, 0)

    barrier = pltpu.get_barrier_semaphore()
    others(
        lambda w, n: pl.semaphore_signal(
            barrier, inc=1, device_id=(w, n), device_id_type=MESH
        )
    )
    table[me] = row_ref[...]
    pl.semaphore_wait(barrier, count - 1)

    def send_row(w, n):
        pltpu.make_async_remote_copy(
            src_ref=row_ref,
            dst_ref=table.at[me],
            send_sem=table_sems.at[0],
            recv_sem=table_sems.at[1],
            device_id=(w, n),
            device_id_type=MESH,
        ).start()

    others(send_row)

    def whole(ref, send_sem, recv_sem):
        part = ref.at[pl.ds(0, count - 1)]
        return pltpu.make_async_remote_copy(
            src_ref=part,
            dst_ref=part,
            send_sem=send_sem,
            recv_sem=recv_sem,
            device_id=(wide, narrow),
            device_id_type=MESH,
        )

    rows = BS * BS * BS // 128
    for f in range(FIELDS):
        loads[f].wait()
        for g in range(blocks // 8):
            for j in range(rows):
                lined[pl.ds(g * 8 * rows + j, 8, stride=rows), :] = raw[
                    f, g * 8 : g * 8 + 8, j * 128 : j * 128 + 128
                ]
        mine[f] = lined[...].reshape(blocks, rows, 128)

    whole(table, table_sems.at[0], table_sems.at[1]).wait_recv()
    local_old = table[...] - me * blocks
    is_mine = (local_old >= 0) & (local_old < blocks)
    chosen = jnp.sum(jnp.where(is_mine, local_old, 0), axis=2, keepdims=True)
    wanted[...] = jnp.broadcast_to(chosen, wanted.shape)
    to_scalar = pltpu.make_async_copy(wanted, wanted_smem, small_sem)
    to_scalar.start()
    to_scalar.wait()

    def block_rows(f, d):
        return mine[f, wanted_smem[d, 0, 0]]

    def send_field(f):
        def send(w, n):
            d = w * narrow_count + n
            stages[f][d] = block_rows(f, d)
            pltpu.make_async_remote_copy(
                src_ref=stages[f].at[d],
                dst_ref=lands[f].at[me],
                send_sem=data_send.at[f],
                recv_sem=data_recv.at[f],
                device_id=(w, n),
                device_id_type=MESH,
            ).start()

        others(send)
        lands[f][me] = block_rows(f, me)

    for f in range(AHEAD):
        send_field(f)

    for load in loads[FIELDS:]:
        load.wait()
    tracers = attr.shape[1]
    chunk = 1024 if tracers % 1024 == 0 else tracers
    means = bin_sums(me * blocks, holder, voxel, attr, blocks, chunk)
    left = lax.broadcasted_iota(jnp.int32, (8, 128), 1) < BINS
    for q in range(blocks // 2):
        pair = means[:, q * 128 : q * 128 + 128]
        across = pltpu.roll(pair, BINS, 1)
        below = pltpu.roll(pair, 4, 0)
        both = pltpu.roll(across, 4, 0)
        mean_mine[2 * q] = jnp.where(left, pair, both)[:4]
        mean_mine[2 * q + 1] = jnp.where(left, across, below)[:4]

    def send_mean(w, n):
        d = w * narrow_count + n
        mean_stage[d] = mean_mine[wanted_smem[d, 0, 0]]
        pltpu.make_async_remote_copy(
            src_ref=mean_stage.at[d],
            dst_ref=mean_land.at[me],
            send_sem=mean_sems.at[0],
            recv_sem=mean_sems.at[1],
            device_id=(w, n),
            device_id_type=MESH,
        ).start()

    others(send_mean)
    mean_land[me] = mean_mine[wanted_smem[me, 0, 0]]

    def source_of(y, z):
        return lax.div(slot_ref[y * LZ + z], blocks)

    def grid_part(f, y):
        for z in range(LZ):
            held[pl.ds(z, rows, stride=LZ), :] = lands[f][source_of(y, z)]
        return swap_groups(held[...].reshape(rows, LZ, 128)).reshape(BS, BS, 128)

    exists = (wide > 0, wide < wide_count - 1, narrow > 0, narrow < narrow_count - 1)
    partner = ((wide - 1, narrow), (wide + 1, narrow), (wide, narrow - 1), (wide, narrow + 1))

    def eta_copy(side, arriving=False):
        if side < 2:
            source = eta_ref.at[1 if side == 0 else nx]
            target = eta_ref.at[nx + 1 if side == 0 else 0]
            mine_at = eta_ref.at[0 if side == 0 else nx + 1]
        else:
            source = eta_out.at[side - 2]
            target = eta_edge_ref.at[3 - side]
            mine_at = eta_edge_ref.at[side - 2]
        return pltpu.make_async_remote_copy(
            src_ref=mine_at if arriving else source,
            dst_ref=mine_at if arriving else target,
            send_sem=eta_send.at[side],
            recv_sem=eta_recv.at[side if arriving else side ^ 1],
            device_id=partner[side],
            device_id_type=MESH,
        )

    def halo_copy(turn, side, arriving=False):
        pad = pads[turn]
        if side < 2:
            source = pad.at[:, 1 if side == 0 else nx]
            target = pad.at[:, nx + 1 if side == 0 else 0]
            mine_at = pad.at[:, 0 if side == 0 else nx + 1]
        else:
            source = edge_out.at[turn, side - 2]
            target = edges[turn].at[3 - side]
            mine_at = edges[turn].at[side - 2]
        return pltpu.make_async_remote_copy(
            src_ref=mine_at if arriving else source,
            dst_ref=mine_at if arriving else target,
            send_sem=halo_send.at[turn, side],
            recv_sem=halo_recv.at[turn, side if arriving else side ^ 1],
            device_id=partner[side],
            device_id_type=MESH,
        )

    def each_side(act, sides=range(4)):
        for side in sides:

            @pl.when(exists[side])
            def _(side=side):
                act(side)

    def viscosity():
        whole(mean_land, mean_sems.at[0], mean_sems.at[1]).wait_recv()
        expand = (
            lax.broadcasted_iota(jnp.int32, (LZ, 32), 0)
            == lax.broadcasted_iota(jnp.int32, (LZ, 32), 1) // 4
        ).astype(jnp.float32)
        same = (
            lax.broadcasted_iota(jnp.int32, (128, 32), 0) % 4
            == lax.broadcasted_iota(jnp.int32, (128, 32), 1) % 4
        )
        gather = (
            lax.broadcasted_iota(jnp.int32, (32, 128), 0)
            == lax.broadcasted_iota(jnp.int32, (32, 128), 1) // 4
        ).astype(jnp.float32)
        for y in range(LY):
            for z in range(LZ):
                mean_held[pl.ds(z, 4, stride=LZ), :] = mean_land[source_of(y, z)]
            for p in range(4):
                tall = jnp.dot(
                    mean_held[p * LZ : p * LZ + LZ].T, expand,
                    precision=lax.Precision.HIGHEST, preferred_element_type=jnp.float32,
                )
                cells = jnp.dot(
                    gather, jnp.where(same, tall, 0.0),
                    precision=lax.Precision.HIGHEST, preferred_element_type=jnp.float32,
                )
                for half in range(2):
                    for layer in range(4):
                        at = half * 16 + layer * 4
                        mean_ref[half * 4 + p, layer, y * 4 : y * 4 + 4, :] = cells[at : at + 4]
        for layer in range(4):
            mixture = MIX_WEIGHTS[0] * mean_ref[0, layer]
            for p in range(1, len(MIX_WEIGHTS)):
                mixture = mixture + MIX_WEIGHTS[p] * mean_ref[p, layer]
            wide_mix = jnp.dot(
                mixture, gather,
                precision=lax.Precision.HIGHEST, preferred_element_type=jnp.float32,
            )
            spread = jnp.concatenate(
                [jnp.broadcast_to(wide_mix[j : j + 1], (4, 128)) for j in range(LY * 4)], axis=0
            )
            for x in range(layer * 4, layer * 4 + 4):
                eta_ref[x + 1] = drag_grid[x] * jnp.exp(
                    HEAT_FACTOR * (0.5 - heat_ref[x]) + spread
                )
        for x in range(nx):
            eta_out[0, x : x + 1] = eta_ref[x + 1, 0:1]
            eta_out[1, x : x + 1] = eta_ref[x + 1, ny - 1 : ny]
        each_side(lambda side: eta_copy(side).start())

    for f in range(FIELDS):
        whole(lands[f], data_send.at[f], data_recv.at[f]).wait_recv()
        if f + AHEAD < FIELDS:
            send_field(f + AHEAD)
        for y in range(LY):
            at = slice(y * BS, (y + 1) * BS)
            part = grid_part(f, y)
            if f == 0:
                heat_ref[:, at, :] = part
            elif f == 1:
                drag_grid[:, at, :] = part
            else:
                pad_0[f - 2, 1 : nx + 1, at, :] = part
        if f == 1:
            viscosity()

    for turn in range(SWEEPS):
        pad = pads[turn]
        each_side(lambda side: halo_copy(turn, side).start(), range(2))
        for k in range(4):
            edge_out[turn, 0, k] = pad[k, 1 : nx + 1, 0, :]
            edge_out[turn, 1, k] = pad[k, 1 : nx + 1, ny - 1, :]
        each_side(lambda side: halo_copy(turn, side).start(), range(2, 4))
        if turn == 0:
            each_side(lambda side: eta_copy(side, True).wait_recv())
        each_side(lambda side: halo_copy(turn, side, True).wait_recv())
        if turn < SWEEPS - 1:

            def slab(x, carry, turn=turn):
                moved = relax_slab(x, eta_ref, eta_edge_ref, pads[turn], edges[turn], heat_ref)
                for k in range(4):
                    pads[turn + 1][k, x + 1] = moved[k]
                return carry

            lax.fori_loop(0, nx, slab, 0)

    whole(table, table_sems.at[0], table_sems.at[1]).wait_send()
    whole(mean_land, mean_sems.at[0], mean_sems.at[1]).wait_send()
    for f in range(FIELDS):
        whole(lands[f], data_send.at[f], data_recv.at[f]).wait_send()
    each_side(lambda side: eta_copy(side).wait_send())
    for turn in range(SWEEPS):
        each_side(lambda side: halo_copy(turn, side).wait_send())


def migrate(row, slots, flow, stress, heat, drag, attributes, holder, voxel):
    wide_count, narrow_count = lax.axis_size("wide"), lax.axis_size("narrow")
    count = wide_count * narrow_count
    blocks = slots.shape[0]
    tracers = attributes.shape[1]
    nx, ny, nz = LX * BS, LY * BS, LZ * BS
    rows = BS * BS * BS // 128
    vmem = pl.BlockSpec(memory_space=pltpu.VMEM)
    smem = pl.BlockSpec(memory_space=pltpu.SMEM)
    hbm = pl.BlockSpec(memory_space=pltpu.HBM)
    f32 = jnp.float32
    per_field = [pltpu.VMEM((count, rows, 128), f32)] * FIELDS
    dma = pltpu.SemaphoreType.DMA
    return pl.pallas_call(
        functools.partial(migrate_kernel, wide_count=wide_count, narrow_count=narrow_count),
        out_shape=(
            jax.ShapeDtypeStruct((4, nx + 2, ny, nz), f32),
            jax.ShapeDtypeStruct((2, 4, nx, nz), f32),
            jax.ShapeDtypeStruct((nx + 2, ny, nz), f32),
            jax.ShapeDtypeStruct((2, nx, nz), f32),
            jax.ShapeDtypeStruct((nx, ny, nz), f32),
            jax.ShapeDtypeStruct((8, LX * 4, LY * 4, LZ * 4), f32),
        ),
        in_specs=[vmem, smem] + [hbm] * 7,
        out_specs=(vmem,) * 6,
        scratch_shapes=[
            pltpu.VMEM((count, 1, 128), jnp.int32),
            pltpu.VMEM((count, 1, 128), jnp.int32),
            pltpu.SMEM((count, 1, 128), jnp.int32),
            pltpu.VMEM((FIELDS, blocks, rows * 128), f32),
            pltpu.VMEM((blocks * rows, 128), f32),
            pltpu.VMEM((FIELDS, blocks, rows, 128), f32),
            *per_field,
            *per_field,
            pltpu.VMEM((8, tracers), f32),
            pltpu.VMEM((1, tracers), jnp.int32),
            pltpu.VMEM((1, tracers), jnp.int32),
            pltpu.VMEM((blocks, 4, 128), f32),
            pltpu.VMEM((count, 4, 128), f32),
            pltpu.VMEM((count, 4, 128), f32),
            pltpu.VMEM((4 * LZ, 128), f32),
            pltpu.VMEM((rows * LZ, 128), f32),
            pltpu.VMEM((nx, ny, nz), f32),
            pltpu.VMEM((4, nx + 2, ny, nz), f32),
            pltpu.VMEM((4, nx + 2, ny, nz), f32),
            pltpu.VMEM((2, 4, nx, nz), f32),
            pltpu.VMEM((2, 4, nx, nz), f32),
            pltpu.VMEM((SWEEPS, 2, 4, nx, nz), f32),
            pltpu.VMEM((2, nx, nz), f32),
            dma((FIELDS + 3,)),
            dma((2,)),
            dma((FIELDS,)),
            dma((FIELDS,)),
            dma((2,)),
            dma((4,)),
            dma((4,)),
            dma((SWEEPS, 4)),
            dma((SWEEPS, 4)),
            dma(()),
        ],
        compiler_params=pltpu.CompilerParams(
            collective_id=1,
            has_side_effects=True,
            vmem_limit_bytes=(24 if count <= 32 else 52) * 1024 * 1024,
        ),
    )(row, slots, flow, stress, heat, drag, attributes, holder, voxel)


def last_kernel(
    pad_ref, edge_ref, eta_ref, eta_edge_ref, heat_ref, mean_ref,
    velocity_ref, pressure_ref, heat_out_ref, mean_out_ref, fresh, sems, *, parts,
):
    nx = heat_ref.shape[0]
    thick = nx // parts
    copies = [
        pltpu.make_async_copy(heat_ref, heat_out_ref, sems.at[2 * parts]),
        pltpu.make_async_copy(mean_ref, mean_out_ref, sems.at[2 * parts + 1]),
    ]
    for copy in copies:
        copy.start()
    for part in range(parts):

        def slab(x, carry):
            moved = relax_slab(x, eta_ref, eta_edge_ref, pad_ref, edge_ref, heat_ref)
            for k in range(4):
                fresh[k, x] = moved[k]
            return carry

        lax.fori_loop(part * thick, (part + 1) * thick, slab, 0)
        at = pl.ds(part * thick, thick)
        copies.append(
            pltpu.make_async_copy(
                fresh.at[pl.ds(0, 3), at], velocity_ref.at[:, at], sems.at[2 * part]
            )
        )
        copies.append(
            pltpu.make_async_copy(fresh.at[3, at], pressure_ref.at[at], sems.at[2 * part + 1])
        )
        for copy in copies[-2:]:
            copy.start()
    for copy in copies:
        copy.wait()


def last_sweep(pad, edge, eta, eta_edge, heat, means):
    nx, ny, nz = heat.shape
    parts = 4
    vmem = pl.BlockSpec(memory_space=pltpu.VMEM)
    hbm = pl.BlockSpec(memory_space=pltpu.HBM)
    return pl.pallas_call(
        functools.partial(last_kernel, parts=parts),
        out_shape=(
            jax.ShapeDtypeStruct((3, nx, ny, nz), jnp.float32),
            jax.ShapeDtypeStruct((nx, ny, nz), jnp.float32),
            jax.ShapeDtypeStruct(heat.shape, jnp.float32),
            jax.ShapeDtypeStruct(means.shape, jnp.float32),
        ),
        in_specs=[vmem] * 6,
        out_specs=(hbm,) * 4,
        scratch_shapes=[
            pltpu.VMEM((4, nx, ny, nz), jnp.float32),
            pltpu.SemaphoreType.DMA((2 * parts + 2,)),
        ],
        compiler_params=pltpu.CompilerParams(vmem_limit_bytes=16 * 1024 * 1024),
    )(pad, edge, eta, eta_edge, heat, means)


def per_device(
    tile_flow_speed,
    tile_stress_mean,
    tile_heat_state,
    tile_drag_coefficient,
    marker_attributes,
    marker_holding_tile,
    marker_voxel_number,
    prior_slot_of_tile,
):
    blocks = prior_slot_of_tile.shape[0]
    tracers = marker_attributes.shape[1]
    row = jnp.pad(prior_slot_of_tile, (0, 128 - blocks), constant_values=-1).reshape(1, 128)
    pad, edge, eta, eta_edge, heat, means = migrate(
        row,
        prior_slot_of_tile,
        tile_flow_speed.transpose(1, 0, 2),
        tile_stress_mean,
        tile_heat_state,
        tile_drag_coefficient,
        marker_attributes,
        marker_holding_tile.reshape(1, tracers),
        marker_voxel_number.reshape(1, tracers),
    )
    return last_sweep(pad, edge, eta, eta_edge, heat, means)


def solution(mesh):
    in_specs = (
        P(("wide", "narrow"), None, None),
        P(("wide", "narrow"), None),
        P(("wide", "narrow"), None),
        P(("wide", "narrow"), None),
        P(None, ("wide", "narrow")),
        P(("wide", "narrow")),
        P(("wide", "narrow")),
        P(("wide", "narrow")),
    )
    out_specs = (
        P(None, "wide", "narrow", None),
        P("wide", "narrow", None),
        P("wide", "narrow", None),
        P(None, "wide", "narrow", None),
    )
    return jax.shard_map(
        per_device, mesh=mesh, in_specs=in_specs, out_specs=out_specs, check_vma=False
    )
```

time: 138 us -> 110 us (0.80)
  Pallas kernels: 114 us -> 101 us
  local copies, waits for them, and re-layouts: 15.4 us -> 7.76 us
  starting transfers between devices: 5.62 us -> 0 us
  other arithmetic: 1.49 us -> 0 us
    pallas_call x8 -> x2, Pallas kernels: 114 us -> 101 us  [the longest x1 98.1 us: migrate(): pl.pallas_call(functools.partial(migrate_kernel, wide_count=wide_count, n...]
    all_to_all x1 -> x0, starting transfers between devices: 5.62 us -> none  [per_device(): lax.all_to_all(outgoing, ('wide', 'narrow'), split_axis=0, concat_axis=0,...]
    unnamed x23 -> x16, local copies, waits for them, and re-layouts: 9.63 us -> 7.1 us
    reshape x6 -> x1, local copies, waits for them, and re-layouts: 3.14 us -> 0.66 us  [per_device(): jnp.pad(prior_slot_of_tile, (0, 128 - blocks), constant_values=-1)]
    transpose x1 -> x0, local copies, waits for them, and re-layouts: 2.12 us -> none  [per_device(): bin_mean_attributes = arrived.transpose(3, 0, 4, 1, 5, 2, 6)]
  transfers between devices with their start and end apart: 1 -> 0, of which waited for: 0 -> 0; matrix products, arithmetic and copies ran while one was open for 5% -> 0% of each run, Pallas kernels for 55% -> 0%
where the time goes in v1:
time: 110 us; the launch traced here: 109 us
  Pallas kernels  101 us (92%)
  local copies, waits for them, and re-layouts  7.76 us (7%)
    pallas_call x1, Pallas kernels, migrate(): pl.pallas_call(functools.partial(migrate_kernel, wide_count=wide_count, n...  98.1 us
    unnamed x16, local copies, waits for them, and re-layouts  7.1 us
    pallas_call x1, Pallas kernels, last_sweep(): pl.pallas_call(functools.partial(last_kernel, parts=parts), out_shape=(ja...  2.8 us

profile of v1, /device:TPU:1, one launch (start us, length us, event | category | flops | bytes accessed | tf_op | source)
XLA Modules:
  0.0 109.3 jit_solution(914326453303944961)
XLA Ops:
  0.6 0.7 pad_bitcast_fusion.row_ref
  1.3 0.0 copy-start
  1.3 1.1 %copy-done = f32[16,3,4096]{2,0,1:T(8,128)S(1)} copy-done((f32[16,3,4096]{2,0,1:T(8,128)S(1)}, f32[16,3,4096]{2,0,1:T(8,128)}, u32[]{:S(2)}) %copy-start) | copy-done | bytes 786456
  2.4 0.0 copy-start.1
  2.4 0.9 copy-done.1
  3.4 0.0 copy-start.2
  3.4 0.9 copy-done.2
  4.3 0.0 copy-start.3
  4.3 0.9 copy-done.3
  5.3 0.0 copy-start.4
  5.3 0.9 copy-done.4
  6.2 0.0 copy-start.5
  6.2 0.8 copy-done.5
  7.0 0.0 copy-start.6
  7.0 0.8 copy-done.6
  7.7 0.0 copy-start.7
  7.7 0.7 copy-done.7
  8.4 98.1 %shard_map.111 = (f32[4,18,32,128]{3,2,1,0:T(8,128)S(1)}, f32[2,4,16,128]{3,2,1,0:T(8,128)S(1)}, f32[18,32,128]{2,1,0:T(8,128)S(1)}, f32[2,16,128]{2,1,0:T(8,128...) custom-call(s32[1,128]{1,0:T(1,128)S(1)} %pad_bitcast_fusion.row_ref, s32[16]{0:T(128)S(1)} %copy-done.7, ...), custom_call_target="tpu_custom_call" | custom-call | tf_op jit(solution)/shard_map/pallas_call | solution.py:444
  106.5 2.8 %shard_map.112 = (f32[3,16,32,128]{3,2,1,0:T(8,128)}, f32[16,32,128]{2,1,0:T(8,128)}, f32[16,32,128]{2,1,0:T(8,128)}, f32[8,4,8,32]{3,2,1,0:T(8,128)}) custom-call(f32[4,18,32,128]{3,2,1,0:T(8,128)S(1)} %get-tuple-element.10.pad_ref, f32[2,4,16,128]{3,2,1,0:T(8,128)S(1)} %get-tuple-element.11.edge_ref, f32[18,32,128]{2,1,0:T(8,128)S(1)} %get-tuple-element.12.eta_ref, ...), custom_call_target="tpu_custom_call" | custom-call | tf_op jit(solution)/shard_map/pallas_call | solution.py:540
Async XLA Ops:
  1.3 1.1 %copy-start = (f32[16,3,4096]{2,0,1:T(8,128)S(1)}, f32[16,3,4096]{2,0,1:T(8,128)}, u32[]{:S(2)}) copy-start(f32[16,3,4096]{2,0,1:T(8,128)} %param.8) | copy-start | bytes 2359300
  2.4 0.9 copy-start.1
  3.4 0.9 copy-start.2
  4.3 0.9 copy-start.3
  5.3 0.9 copy-start.4
  6.2 0.8 copy-start.5
  7.0 0.8 copy-start.6
  7.7 0.7 copy-start.7

commit v2 on v1

--- a/solution.py
+++ b/solution.py
@@ -122,9 +122,9 @@
 
 
 def migrate_kernel(
-    row_ref, slot_ref, flow_ref, stress_ref, warm_ref, drag_ref, attr_ref, holder_ref, voxel_ref,
+    places_ref, flow_ref, stress_ref, warm_ref, drag_ref, attr_ref, holder_ref, voxel_ref,
     pad_ref, edge_ref, eta_ref, eta_edge_ref, heat_ref, mean_ref,
-    table, wanted, wanted_smem, raw, lined, mine, stage_0, stage_1, stage_2, stage_3, stage_4, stage_5,
+    slot_ref, row_ref, table, wanted, wanted_smem, raw, lined, mine, stage_0, stage_1, stage_2, stage_3, stage_4, stage_5,
     land_0, land_1, land_2, land_3, land_4, land_5,
     attr, holder, voxel, mean_mine, mean_stage, mean_land, mean_held, held, drag_grid,
     pad_0, pad_1, edge_0, edge_1, edge_out, eta_out,
@@ -142,6 +142,8 @@
     pads = (pad_0, pad_1, pad_ref)
     edges = (edge_0, edge_1, edge_ref)
 
+    to_slots = pltpu.make_async_copy(places_ref, slot_ref, small_sem)
+    to_slots.start()
     sources = (
         warm_ref, drag_ref, flow_ref.at[0], flow_ref.at[1], flow_ref.at[2], stress_ref,
     )
@@ -182,7 +184,13 @@
             barrier, inc=1, device_id=(w, n), device_id_type=MESH
         )
     )
-    table[me] = row_ref[...]
+    to_slots.wait()
+    lane = lax.broadcasted_iota(jnp.int32, (1, 128), 1)
+    places = jnp.full((1, 128), -1, jnp.int32)
+    for r in range(blocks):
+        places = jnp.where(lane == r, slot_ref[r], places)
+    row_ref[...] = places
+    table[me] = places
     pl.semaphore_wait(barrier, count - 1)
 
     def send_row(w, n):
@@ -428,7 +436,7 @@
         each_side(lambda side: halo_copy(turn, side).wait_send())
 
 
-def migrate(row, slots, flow, stress, heat, drag, attributes, holder, voxel):
+def migrate(slots, flow, stress, heat, drag, attributes, holder, voxel):
     wide_count, narrow_count = lax.axis_size("wide"), lax.axis_size("narrow")
     count = wide_count * narrow_count
     blocks = slots.shape[0]
@@ -436,11 +444,14 @@
     nx, ny, nz = LX * BS, LY * BS, LZ * BS
     rows = BS * BS * BS // 128
     vmem = pl.BlockSpec(memory_space=pltpu.VMEM)
-    smem = pl.BlockSpec(memory_space=pltpu.SMEM)
     hbm = pl.BlockSpec(memory_space=pltpu.HBM)
     f32 = jnp.float32
     per_field = [pltpu.VMEM((count, rows, 128), f32)] * FIELDS
     dma = pltpu.SemaphoreType.DMA
+    pinned = [
+        pltpu.with_memory_space_constraint(array, pltpu.HBM)
+        for array in (slots, flow, stress, heat, drag, attributes, holder, voxel)
+    ]
     return pl.pallas_call(
         functools.partial(migrate_kernel, wide_count=wide_count, narrow_count=narrow_count),
         out_shape=(
@@ -451,9 +462,11 @@
             jax.ShapeDtypeStruct((nx, ny, nz), f32),
             jax.ShapeDtypeStruct((8, LX * 4, LY * 4, LZ * 4), f32),
         ),
-        in_specs=[vmem, smem] + [hbm] * 7,
+        in_specs=[hbm] * 8,
         out_specs=(vmem,) * 6,
         scratch_shapes=[
+            pltpu.SMEM((blocks,), jnp.int32),
+            pltpu.VMEM((1, 128), jnp.int32),
             pltpu.VMEM((count, 1, 128), jnp.int32),
             pltpu.VMEM((count, 1, 128), jnp.int32),
             pltpu.SMEM((count, 1, 128), jnp.int32),
@@ -493,7 +506,7 @@
             has_side_effects=True,
             vmem_limit_bytes=(24 if count <= 32 else 52) * 1024 * 1024,
         ),
-    )(row, slots, flow, stress, heat, drag, attributes, holder, voxel)
+    )(*pinned)
 
 
 def last_kernel(
@@ -565,11 +578,8 @@
     marker_voxel_number,
     prior_slot_of_tile,
 ):
-    blocks = prior_slot_of_tile.shape[0]
     tracers = marker_attributes.shape[1]
-    row = jnp.pad(prior_slot_of_tile, (0, 128 - blocks), constant_values=-1).reshape(1, 128)
     pad, edge, eta, eta_edge, heat, means = migrate(
-        row,
         prior_slot_of_tile,
         tile_flow_speed.transpose(1, 0, 2),
         tile_stress_mean,

time: 110 us -> 101 us (0.918)
  local copies, waits for them, and re-layouts: 7.76 us -> 0 us
    unnamed x16 -> x0, local copies, waits for them, and re-layouts: 7.1 us -> none
where the time goes in v2:
time: 101 us
  Pallas kernels  100 us (99%)
    pallas_call x1, Pallas kernels, migrate(): pl.pallas_call(functools.partial(migrate_kernel, wide_count=wide_count, n...  97.4 us
    pallas_call x1, Pallas kernels, last_sweep(): pl.pallas_call(functools.partial(last_kernel, parts=parts), out_shape=(ja...  2.77 us

profile of v2, /device:TPU:1, one launch (start us, length us, event | category | flops | bytes accessed | tf_op | source)
XLA Modules:
  0.0 100.8 jit_solution(11050512486893954260)
XLA Ops:
  0.6 97.4 %shard_map.111 = (f32[4,18,32,128]{3,2,1,0:T(8,128)S(1)}, f32[2,4,16,128]{3,2,1,0:T(8,128)S(1)}, f32[18,32,128]{2,1,0:T(8,128)S(1)}, f32[2,16,128]{2,1,0:T(8,128...) custom-call(s32[16]{0:T(128)} %places_ref.1, f32[3,16,4096]{2,1,0:T(8,128)} %bitcast.3, ...), custom_call_target="tpu_custom_call" | custom-call | tf_op jit(solution)/shard_map/pallas_call | solution.py:455
  98.0 2.8 %shard_map.112 = (f32[3,16,32,128]{3,2,1,0:T(8,128)}, f32[16,32,128]{2,1,0:T(8,128)}, f32[16,32,128]{2,1,0:T(8,128)}, f32[8,4,8,32]{3,2,1,0:T(8,128)}) custom-call(f32[4,18,32,128]{3,2,1,0:T(8,128)S(1)} %get-tuple-element.10.pad_ref, f32[2,4,16,128]{3,2,1,0:T(8,128)S(1)} %get-tuple-element.11.edge_ref, f32[18,32,128]{2,1,0:T(8,128)S(1)} %get-tuple-element.12.eta_ref, ...), custom_call_target="tpu_custom_call" | custom-call | tf_op jit(solution)/shard_map/pallas_call | solution.py:553

commit v3 on v2

--- a/solution.py
+++ b/solution.py
@@ -15,6 +15,8 @@
 BINS = 64
 FIELDS = 6
 AHEAD = 3
+PITCH = 40
+FIRST = 8
 
 MIX_WEIGHTS = (0.3, -0.25, 0.2, -0.15, 0.35, -0.3, 0.25, -0.2)
 RELAX_WEIGHT = 0.7
@@ -71,63 +73,92 @@
     return total / jnp.maximum(sums[3 * props :], 1.0)
 
 
-def relax_slab(x, eta_pad, eta_edges, pad, edges, heat_ref):
-    ny, nz = heat_ref.shape[1:]
-    row = lax.broadcasted_iota(jnp.int32, (ny, nz), 0)
-    column = lax.broadcasted_iota(jnp.int32, (ny, nz), 1)
-
-    def around(here, lower, upper, low, high):
-        return (
-            here,
-            upper,
-            lower,
-            jnp.where(row == ny - 1, high, pltpu.roll(here, ny - 1, 0)),
-            jnp.where(row == 0, low, pltpu.roll(here, 1, 0)),
-            jnp.where(column == nz - 1, 0.0, pltpu.roll(here, nz - 1, 1)),
-            jnp.where(column == 0, 0.0, pltpu.roll(here, 1, 1)),
-        )
-
-    def field(k):
-        return around(
-            pad[k, x + 1], pad[k, x], pad[k, x + 2],
-            edges[0, k, pl.ds(x, 1), :], edges[1, k, pl.ds(x, 1), :],
-        )
-
-    eta = around(
-        eta_pad[x + 1], eta_pad[x], eta_pad[x + 2],
-        eta_edges[0, pl.ds(x, 1), :], eta_edges[1, pl.ds(x, 1), :],
-    )
-    face = [0.5 * (eta[0] + eta[m]) for m in range(1, 7)]
+def at_ends(shape):
+    column = lax.broadcasted_iota(jnp.int32, shape, 1)
+    return column == 0, column == shape[1] - 1
+
+
+def z_pair(here):
+    low_end, high_end = at_ends(here.shape)
+    nz = here.shape[1]
+    return (
+        jnp.where(high_end, 0.0, pltpu.roll(here, nz - 1, 1)),
+        jnp.where(low_end, 0.0, pltpu.roll(here, 1, 1)),
+    )
+
+
+def factors(x, eta_ref, heat_ref, side_ref, rest_ref):
+    ny = heat_ref.shape[1]
+    base = pl.multiple_of((x + 1) * PITCH + FIRST, 8)
+    here = eta_ref[pl.ds(base, ny), :]
+    around = [
+        eta_ref[pl.ds(base + off, ny), :] for off in (PITCH, -PITCH, 1, -1)
+    ] + list(z_pair(here))
+    face = [0.5 * (here + other) for other in around]
     diagonal = face[0]
     for m in range(1, 6):
         diagonal = diagonal + face[m]
     scale = RELAX_WEIGHT / diagonal
-    press = field(3)
+    low_end, high_end = at_ends(here.shape)
+    for m in range(6):
+        value = face[m] * scale
+        if m == 4:
+            value = jnp.where(high_end, 0.0, value)
+        elif m == 5:
+            value = jnp.where(low_end, 0.0, value)
+        side_ref[m, x] = value
+    rest_ref[0, x] = 0.5 * scale
+    rest_ref[1, x] = (0.5 * PRESSURE_WEIGHT) * here
+    rest_ref[2, x] = scale * (DENSITY_FACTOR * heat_ref[x])
+
+
+def relax(x, first, rows, pad, side_ref, rest_ref):
+    base = (x + 1) * PITCH + FIRST + first
+    nz = pad.shape[2]
+    own = pl.ds(first, rows)
+
+    def value(k, off=0):
+        return pad[k, pl.ds(base + off, rows), :]
+
+    side = [side_ref[m, x, own, :] for m in range(6)]
+    half_scale, squeeze, lift = (rest_ref[m, x, own, :] for m in range(3))
+    press = value(3)
+    press_up_z, press_down_z = z_pair(press)
+    drops = (
+        value(3, PITCH) - value(3, -PITCH),
+        value(3, 1) - value(3, -1),
+        press_up_z - press_down_z,
+    )
+    moved = []
     divergence = None
-    moved = []
-    for component in range(3):
-        speed = field(component)
-        residual = face[0] * (speed[1] - speed[0])
-        for m in range(1, 6):
-            residual = residual + face[m] * (speed[m + 1] - speed[0])
-        up, down = 2 * component + 1, 2 * component + 2
-        residual = residual - 0.5 * (press[up] - press[down])
-        if component == 2:
-            residual = residual + DENSITY_FACTOR * heat_ref[x]
-        moved.append(speed[0] + residual * scale)
-        flux = 0.5 * (speed[up] - speed[down])
+    for k in range(3):
+        here = value(k)
+        if k == 2:
+            up_z, down_z = z_pair(here)
+        else:
+            up_z, down_z = pltpu.roll(here, nz - 1, 1), pltpu.roll(here, 1, 1)
+        near = (
+            value(k, PITCH), value(k, -PITCH), value(k, 1), value(k, -1), up_z, down_z,
+        )
+        fresh = (1.0 - RELAX_WEIGHT) * here - half_scale * drops[k]
+        for m in range(6):
+            fresh = fresh + side[m] * near[m]
+        if k == 2:
+            fresh = fresh + lift
+        moved.append(fresh)
+        flux = near[2 * k] - near[2 * k + 1]
         divergence = flux if divergence is None else divergence + flux
-    moved.append(press[0] - PRESSURE_WEIGHT * eta[0] * divergence)
+    moved.append(press - squeeze * divergence)
     return moved
 
 
 def migrate_kernel(
     places_ref, flow_ref, stress_ref, warm_ref, drag_ref, attr_ref, holder_ref, voxel_ref,
-    pad_ref, edge_ref, eta_ref, eta_edge_ref, heat_ref, mean_ref,
-    slot_ref, row_ref, table, wanted, wanted_smem, raw, lined, mine, stage_0, stage_1, stage_2, stage_3, stage_4, stage_5,
+    pad_ref, inner_ref, side_ref, rest_ref, heat_ref, mean_ref,
+    slot_ref, row_ref, table, table_smem, raw, lined, mine, stage_0, stage_1, stage_2, stage_3, stage_4, stage_5,
     land_0, land_1, land_2, land_3, land_4, land_5,
     attr, holder, voxel, mean_mine, mean_stage, mean_land, mean_held, held, drag_grid,
-    pad_0, pad_1, edge_0, edge_1, edge_out, eta_out,
+    pad_0, pad_1, eta, edge_in, edge_out, eta_in, eta_out,
     raw_sems, table_sems, data_send, data_recv, mean_sems,
     eta_send, eta_recv, halo_send, halo_recv, small_sem,
     *, wide_count, narrow_count,
@@ -140,7 +171,6 @@
     stages = (stage_0, stage_1, stage_2, stage_3, stage_4, stage_5)
     lands = (land_0, land_1, land_2, land_3, land_4, land_5)
     pads = (pad_0, pad_1, pad_ref)
-    edges = (edge_0, edge_1, edge_ref)
 
     to_slots = pltpu.make_async_copy(places_ref, slot_ref, small_sem)
     to_slots.start()
@@ -156,15 +186,6 @@
     for load in loads:
         load.start()
 
-    for pad in pads:
-        for x in (0, nx + 1):
-            pad[:, x] = jnp.zeros((4, ny, nz), jnp.float32)
-    for x in (0, nx + 1):
-        eta_ref[x] = jnp.zeros((ny, nz), jnp.float32)
-    for edge in edges:
-        edge[...] = jnp.zeros(edge.shape, jnp.float32)
-    eta_edge_ref[...] = jnp.zeros(eta_edge_ref.shape, jnp.float32)
-
     def others(act):
         near = [lax.rem(narrow + b, narrow_count) for b in range(narrow_count)]
         for b in range(1, narrow_count):
@@ -186,9 +207,13 @@
     )
     to_slots.wait()
     lane = lax.broadcasted_iota(jnp.int32, (1, 128), 1)
-    places = jnp.full((1, 128), -1, jnp.int32)
+    places = jnp.zeros((1, 128), jnp.int32)
+    my_own = jnp.int32(0)
     for r in range(blocks):
-        places = jnp.where(lane == r, slot_ref[r], places)
+        owner = lax.div(slot_ref[r], blocks)
+        local = slot_ref[r] - owner * blocks
+        places = jnp.where(lane == owner, local, places)
+        my_own = jnp.where(owner == me, local, my_own)
     row_ref[...] = places
     table[me] = places
     pl.semaphore_wait(barrier, count - 1)
@@ -205,6 +230,12 @@
 
     others(send_row)
 
+    for pad in pads:
+        pad[...] = jnp.zeros(pad.shape, jnp.float32)
+    eta[...] = jnp.zeros(eta.shape, jnp.float32)
+    edge_in[...] = jnp.zeros(edge_in.shape, jnp.float32)
+    eta_in[...] = jnp.zeros(eta_in.shape, jnp.float32)
+
     def whole(ref, send_sem, recv_sem):
         part = ref.at[pl.ds(0, count - 1)]
         return pltpu.make_async_remote_copy(
@@ -227,21 +258,17 @@
         mine[f] = lined[...].reshape(blocks, rows, 128)
 
     whole(table, table_sems.at[0], table_sems.at[1]).wait_recv()
-    local_old = table[...] - me * blocks
-    is_mine = (local_old >= 0) & (local_old < blocks)
-    chosen = jnp.sum(jnp.where(is_mine, local_old, 0), axis=2, keepdims=True)
-    wanted[...] = jnp.broadcast_to(chosen, wanted.shape)
-    to_scalar = pltpu.make_async_copy(wanted, wanted_smem, small_sem)
+    to_scalar = pltpu.make_async_copy(table, table_smem, small_sem)
     to_scalar.start()
     to_scalar.wait()
 
-    def block_rows(f, d):
-        return mine[f, wanted_smem[d, 0, 0]]
+    def wanted(d):
+        return table_smem[d, 0, me]
 
     def send_field(f):
         def send(w, n):
             d = w * narrow_count + n
-            stages[f][d] = block_rows(f, d)
+            stages[f][d] = mine[f, wanted(d)]
             pltpu.make_async_remote_copy(
                 src_ref=stages[f].at[d],
                 dst_ref=lands[f].at[me],
@@ -252,7 +279,7 @@
             ).start()
 
         others(send)
-        lands[f][me] = block_rows(f, me)
+        lands[f][me] = mine[f, my_own]
 
     for f in range(AHEAD):
         send_field(f)
@@ -273,7 +300,7 @@
 
     def send_mean(w, n):
         d = w * narrow_count + n
-        mean_stage[d] = mean_mine[wanted_smem[d, 0, 0]]
+        mean_stage[d] = mean_mine[wanted(d)]
         pltpu.make_async_remote_copy(
             src_ref=mean_stage.at[d],
             dst_ref=mean_land.at[me],
@@ -284,7 +311,7 @@
         ).start()
 
     others(send_mean)
-    mean_land[me] = mean_mine[wanted_smem[me, 0, 0]]
+    mean_land[me] = mean_mine[my_own]
 
     def source_of(y, z):
         return lax.div(slot_ref[y * LZ + z], blocks)
@@ -297,15 +324,24 @@
     exists = (wide > 0, wide < wide_count - 1, narrow > 0, narrow < narrow_count - 1)
     partner = ((wide - 1, narrow), (wide + 1, narrow), (wide, narrow - 1), (wide, narrow + 1))
 
+    def slab_rows(x):
+        return pl.ds(x * PITCH + FIRST, ny)
+
+    def edge_rows(side):
+        return pl.ds(PITCH + FIRST + (0 if side == 2 else ny - 1), nx, stride=PITCH)
+
+    def beside_rows(side):
+        return pl.ds(PITCH + FIRST + (-1 if side == 2 else ny), nx, stride=PITCH)
+
     def eta_copy(side, arriving=False):
         if side < 2:
-            source = eta_ref.at[1 if side == 0 else nx]
-            target = eta_ref.at[nx + 1 if side == 0 else 0]
-            mine_at = eta_ref.at[0 if side == 0 else nx + 1]
+            source = eta.at[slab_rows(1 if side == 0 else nx)]
+            target = eta.at[slab_rows(nx + 1 if side == 0 else 0)]
+            mine_at = eta.at[slab_rows(0 if side == 0 else nx + 1)]
         else:
             source = eta_out.at[side - 2]
-            target = eta_edge_ref.at[3 - side]
-            mine_at = eta_edge_ref.at[side - 2]
+            target = eta_in.at[3 - side]
+            mine_at = eta_in.at[side - 2]
         return pltpu.make_async_remote_copy(
             src_ref=mine_at if arriving else source,
             dst_ref=mine_at if arriving else target,
@@ -315,21 +351,25 @@
             device_id_type=MESH,
         )
 
-    def halo_copy(turn, side, arriving=False):
+    groups = ((0, 0, 1), (0, 1, 1), (0, 2, 1), (0, 3, 1), (1, 0, 4), (2, 0, 4))
+
+    def halo_copy(group, side, arriving=False):
+        turn, first, fields = groups[group]
+        ks = pl.ds(first, fields)
         pad = pads[turn]
         if side < 2:
-            source = pad.at[:, 1 if side == 0 else nx]
-            target = pad.at[:, nx + 1 if side == 0 else 0]
-            mine_at = pad.at[:, 0 if side == 0 else nx + 1]
+            source = pad.at[ks, slab_rows(1 if side == 0 else nx)]
+            target = pad.at[ks, slab_rows(nx + 1 if side == 0 else 0)]
+            mine_at = pad.at[ks, slab_rows(0 if side == 0 else nx + 1)]
         else:
-            source = edge_out.at[turn, side - 2]
-            target = edges[turn].at[3 - side]
-            mine_at = edges[turn].at[side - 2]
+            source = edge_out.at[turn, side - 2, ks]
+            target = edge_in.at[turn, 3 - side, ks]
+            mine_at = edge_in.at[turn, side - 2, ks]
         return pltpu.make_async_remote_copy(
             src_ref=mine_at if arriving else source,
             dst_ref=mine_at if arriving else target,
-            send_sem=halo_send.at[turn, side],
-            recv_sem=halo_recv.at[turn, side if arriving else side ^ 1],
+            send_sem=halo_send.at[group, side],
+            recv_sem=halo_recv.at[group, side if arriving else side ^ 1],
             device_id=partner[side],
             device_id_type=MESH,
         )
@@ -340,6 +380,21 @@
             @pl.when(exists[side])
             def _(side=side):
                 act(side)
+
+    def send_halo(group):
+        turn, first, fields = groups[group]
+        each_side(lambda side: halo_copy(group, side).start(), range(2))
+        for k in range(first, first + fields):
+            for side in (2, 3):
+                edge_out[turn, side - 2, k] = pads[turn][k, edge_rows(side), :]
+        each_side(lambda side: halo_copy(group, side).start(), range(2, 4))
+
+    def take_halo(group):
+        turn, first, fields = groups[group]
+        each_side(lambda side: halo_copy(group, side, True).wait_recv())
+        for k in range(first, first + fields):
+            for side in (2, 3):
+                pads[turn][k, beside_rows(side), :] = edge_in[turn, side - 2, k]
 
     def viscosity():
         whole(mean_land, mean_sems.at[0], mean_sems.at[1]).wait_recv()
@@ -383,13 +438,23 @@
                 [jnp.broadcast_to(wide_mix[j : j + 1], (4, 128)) for j in range(LY * 4)], axis=0
             )
             for x in range(layer * 4, layer * 4 + 4):
-                eta_ref[x + 1] = drag_grid[x] * jnp.exp(
+                eta[slab_rows(x + 1), :] = drag_grid[x] * jnp.exp(
                     HEAT_FACTOR * (0.5 - heat_ref[x]) + spread
                 )
-        for x in range(nx):
-            eta_out[0, x : x + 1] = eta_ref[x + 1, 0:1]
-            eta_out[1, x : x + 1] = eta_ref[x + 1, ny - 1 : ny]
+        for side in (2, 3):
+            eta_out[side - 2] = eta[edge_rows(side), :]
         each_side(lambda side: eta_copy(side).start())
+
+    def take_eta():
+        each_side(lambda side: eta_copy(side, True).wait_recv())
+        for side in (2, 3):
+            eta[beside_rows(side), :] = eta_in[side - 2]
+
+        def slab(x, carry):
+            factors(x, eta, heat_ref, side_ref, rest_ref)
+            return carry
+
+        lax.fori_loop(0, nx, slab, 0)
 
     for f in range(FIELDS):
         whole(lands[f], data_send.at[f], data_recv.at[f]).wait_recv()
@@ -403,37 +468,46 @@
             elif f == 1:
                 drag_grid[:, at, :] = part
             else:
-                pad_0[f - 2, 1 : nx + 1, at, :] = part
+                for x in range(nx):
+                    pad_0[f - 2, pl.ds((x + 1) * PITCH + FIRST + y * BS, BS), :] = part[x]
         if f == 1:
             viscosity()
+        elif f > 1:
+            send_halo(f - 2)
+        if f == 3:
+            take_eta()
+
+    def sweep(turn, first_x, end_x, first, rows):
+        def slab(x, carry):
+            moved = relax(x, first, rows, pads[turn], side_ref, rest_ref)
+            for k in range(4):
+                if turn == SWEEPS - 1:
+                    inner_ref[k, x - 1] = moved[k]
+                else:
+                    pads[turn + 1][k, pl.ds((x + 1) * PITCH + FIRST + first, rows), :] = moved[k]
+            return carry
+
+        lax.fori_loop(first_x, end_x, slab, 0)
 
     for turn in range(SWEEPS):
-        pad = pads[turn]
-        each_side(lambda side: halo_copy(turn, side).start(), range(2))
-        for k in range(4):
-            edge_out[turn, 0, k] = pad[k, 1 : nx + 1, 0, :]
-            edge_out[turn, 1, k] = pad[k, 1 : nx + 1, ny - 1, :]
-        each_side(lambda side: halo_copy(turn, side).start(), range(2, 4))
-        if turn == 0:
-            each_side(lambda side: eta_copy(side, True).wait_recv())
-        each_side(lambda side: halo_copy(turn, side, True).wait_recv())
+        if turn > 0:
+            send_halo(3 + turn)
+        sweep(turn, 1, nx - 1, 8, ny - 16)
+        for group in range(4) if turn == 0 else (3 + turn,):
+            take_halo(group)
         if turn < SWEEPS - 1:
-
-            def slab(x, carry, turn=turn):
-                moved = relax_slab(x, eta_ref, eta_edge_ref, pads[turn], edges[turn], heat_ref)
-                for k in range(4):
-                    pads[turn + 1][k, x + 1] = moved[k]
-                return carry
-
-            lax.fori_loop(0, nx, slab, 0)
+            sweep(turn, 0, 1, 0, ny)
+            sweep(turn, nx - 1, nx, 0, ny)
+            sweep(turn, 1, nx - 1, 0, 8)
+            sweep(turn, 1, nx - 1, ny - 8, 8)
 
     whole(table, table_sems.at[0], table_sems.at[1]).wait_send()
     whole(mean_land, mean_sems.at[0], mean_sems.at[1]).wait_send()
     for f in range(FIELDS):
         whole(lands[f], data_send.at[f], data_recv.at[f]).wait_send()
     each_side(lambda side: eta_copy(side).wait_send())
-    for turn in range(SWEEPS):
-        each_side(lambda side: halo_copy(turn, side).wait_send())
+    for group in range(len(groups)):
+        each_side(lambda side: halo_copy(group, side).wait_send())
 
 
 def migrate(slots, flow, stress, heat, drag, attributes, holder, voxel):
@@ -443,6 +517,7 @@
     tracers = attributes.shape[1]
     nx, ny, nz = LX * BS, LY * BS, LZ * BS
     rows = BS * BS * BS // 128
+    pad_rows = (nx + 2) * PITCH + 8
     vmem = pl.BlockSpec(memory_space=pltpu.VMEM)
     hbm = pl.BlockSpec(memory_space=pltpu.HBM)
     f32 = jnp.float32
@@ -455,10 +530,10 @@
     return pl.pallas_call(
         functools.partial(migrate_kernel, wide_count=wide_count, narrow_count=narrow_count),
         out_shape=(
-            jax.ShapeDtypeStruct((4, nx + 2, ny, nz), f32),
-            jax.ShapeDtypeStruct((2, 4, nx, nz), f32),
-            jax.ShapeDtypeStruct((nx + 2, ny, nz), f32),
-            jax.ShapeDtypeStruct((2, nx, nz), f32),
+            jax.ShapeDtypeStruct((4, pad_rows, nz), f32),
+            jax.ShapeDtypeStruct((4, nx - 2, ny - 16, nz), f32),
+            jax.ShapeDtypeStruct((6, nx, ny, nz), f32),
+            jax.ShapeDtypeStruct((3, nx, ny, nz), f32),
             jax.ShapeDtypeStruct((nx, ny, nz), f32),
             jax.ShapeDtypeStruct((8, LX * 4, LY * 4, LZ * 4), f32),
         ),
@@ -467,7 +542,6 @@
         scratch_shapes=[
             pltpu.SMEM((blocks,), jnp.int32),
             pltpu.VMEM((1, 128), jnp.int32),
-            pltpu.VMEM((count, 1, 128), jnp.int32),
             pltpu.VMEM((count, 1, 128), jnp.int32),
             pltpu.SMEM((count, 1, 128), jnp.int32),
             pltpu.VMEM((FIELDS, blocks, rows * 128), f32),
@@ -484,11 +558,12 @@
             pltpu.VMEM((4 * LZ, 128), f32),
             pltpu.VMEM((rows * LZ, 128), f32),
             pltpu.VMEM((nx, ny, nz), f32),
-            pltpu.VMEM((4, nx + 2, ny, nz), f32),
-            pltpu.VMEM((4, nx + 2, ny, nz), f32),
-            pltpu.VMEM((2, 4, nx, nz), f32),
-            pltpu.VMEM((2, 4, nx, nz), f32),
+            pltpu.VMEM((4, pad_rows, nz), f32),
+            pltpu.VMEM((4, pad_rows, nz), f32),
+            pltpu.VMEM((pad_rows, nz), f32),
             pltpu.VMEM((SWEEPS, 2, 4, nx, nz), f32),
+            pltpu.VMEM((SWEEPS, 2, 4, nx, nz), f32),
+            pltpu.VMEM((2, nx, nz), f32),
             pltpu.VMEM((2, nx, nz), f32),
             dma((FIELDS + 3,)),
             dma((2,)),
@@ -497,8 +572,8 @@
             dma((2,)),
             dma((4,)),
             dma((4,)),
-            dma((SWEEPS, 4)),
-            dma((SWEEPS, 4)),
+            dma((SWEEPS + 3, 4)),
+            dma((SWEEPS + 3, 4)),
             dma(()),
         ],
         compiler_params=pltpu.CompilerParams(
@@ -510,48 +585,51 @@
 
 
 def last_kernel(
-    pad_ref, edge_ref, eta_ref, eta_edge_ref, heat_ref, mean_ref,
-    velocity_ref, pressure_ref, heat_out_ref, mean_out_ref, fresh, sems, *, parts,
+    pad_ref, inner_ref, side_ref, rest_ref, heat_ref, mean_ref,
+    velocity_ref, pressure_ref, heat_out_ref, mean_out_ref, fresh, sems,
 ):
-    nx = heat_ref.shape[0]
-    thick = nx // parts
-    copies = [
-        pltpu.make_async_copy(heat_ref, heat_out_ref, sems.at[2 * parts]),
-        pltpu.make_async_copy(mean_ref, mean_out_ref, sems.at[2 * parts + 1]),
-    ]
-    for copy in copies:
-        copy.start()
-    for part in range(parts):
-
+    nx, ny, nz = heat_ref.shape
+    copies = []
+
+    def send(source, target):
+        copies.append(pltpu.make_async_copy(source, target, sems.at[len(copies)]))
+        copies[-1].start()
+
+    def send_fresh(xs, ys):
+        send(fresh.at[pl.ds(0, 3), xs, ys], velocity_ref.at[:, xs, ys])
+        send(fresh.at[3, xs, ys], pressure_ref.at[xs, ys])
+
+    send(heat_ref, heat_out_ref)
+    send(mean_ref, mean_out_ref)
+    middle, centre = pl.ds(1, nx - 2), pl.ds(8, ny - 16)
+    send(inner_ref.at[pl.ds(0, 3)], velocity_ref.at[:, middle, centre])
+    send(inner_ref.at[3], pressure_ref.at[middle, centre])
+
+    def sweep(first_x, end_x, first, rows):
         def slab(x, carry):
-            moved = relax_slab(x, eta_ref, eta_edge_ref, pad_ref, edge_ref, heat_ref)
+            moved = relax(x, first, rows, pad_ref, side_ref, rest_ref)
             for k in range(4):
-                fresh[k, x] = moved[k]
+                fresh[k, x, pl.ds(first, rows), :] = moved[k]
             return carry
 
-        lax.fori_loop(part * thick, (part + 1) * thick, slab, 0)
-        at = pl.ds(part * thick, thick)
-        copies.append(
-            pltpu.make_async_copy(
-                fresh.at[pl.ds(0, 3), at], velocity_ref.at[:, at], sems.at[2 * part]
-            )
-        )
-        copies.append(
-            pltpu.make_async_copy(fresh.at[3, at], pressure_ref.at[at], sems.at[2 * part + 1])
-        )
-        for copy in copies[-2:]:
-            copy.start()
+        lax.fori_loop(first_x, end_x, slab, 0)
+
+    for first in (0, ny - 8):
+        sweep(1, nx - 1, first, 8)
+        send_fresh(middle, pl.ds(first, 8))
+    for x in (0, nx - 1):
+        sweep(x, x + 1, 0, ny)
+        send_fresh(pl.ds(x, 1), pl.ds(0, ny))
     for copy in copies:
         copy.wait()
 
 
-def last_sweep(pad, edge, eta, eta_edge, heat, means):
+def last_sweep(pad, inner, side, rest, heat, means):
     nx, ny, nz = heat.shape
-    parts = 4
     vmem = pl.BlockSpec(memory_space=pltpu.VMEM)
     hbm = pl.BlockSpec(memory_space=pltpu.HBM)
     return pl.pallas_call(
-        functools.partial(last_kernel, parts=parts),
+        last_kernel,
         out_shape=(
             jax.ShapeDtypeStruct((3, nx, ny, nz), jnp.float32),
             jax.ShapeDtypeStruct((nx, ny, nz), jnp.float32),
@@ -562,10 +640,10 @@
         out_specs=(hbm,) * 4,
         scratch_shapes=[
             pltpu.VMEM((4, nx, ny, nz), jnp.float32),
-            pltpu.SemaphoreType.DMA((2 * parts + 2,)),
+            pltpu.SemaphoreType.DMA((12,)),
         ],
         compiler_params=pltpu.CompilerParams(vmem_limit_bytes=16 * 1024 * 1024),
-    )(pad, edge, eta, eta_edge, heat, means)
+    )(pad, inner, side, rest, heat, means)
 
 
 def per_device(
@@ -579,7 +657,7 @@
     prior_slot_of_tile,
 ):
     tracers = marker_attributes.shape[1]
-    pad, edge, eta, eta_edge, heat, means = migrate(
+    results = migrate(
         prior_slot_of_tile,
         tile_flow_speed.transpose(1, 0, 2),
         tile_stress_mean,
@@ -589,7 +667,7 @@
         marker_holding_tile.reshape(1, tracers),
         marker_voxel_number.reshape(1, tracers),
     )
-    return last_sweep(pad, edge, eta, eta_edge, heat, means)
+    return last_sweep(*results)
 
 
 def solution(mesh):

time: 101 us -> 102 us (level)
  Pallas kernels: 100 us -> 102 us
where the time goes in v3:
time: 102 us
  Pallas kernels  102 us (100%)
    pallas_call x1, Pallas kernels, migrate(): pl.pallas_call(functools.partial(migrate_kernel, wide_count=wide_count, n...  98.3 us
    pallas_call x1, Pallas kernels, last_sweep(): pl.pallas_call(last_kernel, out_shape=(jax.ShapeDtypeStruct((3, nx, ny, n...  3.22 us

profile of v3, /device:TPU:1, one launch (start us, length us, event | category | flops | bytes accessed | tf_op | source)
XLA Modules:
  0.0 102.2 jit_solution(5423577170881238864)
XLA Ops:
  0.6 98.3 %shard_map.111 = (f32[4,728,128]{2,1,0:T(8,128)S(1)}, f32[4,14,16,128]{3,2,1,0:T(8,128)S(1)}, f32[6,16,32,128]{3,2,1,0:T(8,128)S(1)}, f32[3,16,32,128]{3,2,1,0:T...) custom-call(s32[16]{0:T(128)} %places_ref.1, f32[3,16,4096]{2,1,0:T(8,128)} %bitcast.3, ...), custom_call_target="tpu_custom_call" | custom-call | tf_op jit(solution)/shard_map/pallas_call | solution.py:530
  98.9 3.2 %shard_map.112 = (f32[3,16,32,128]{3,2,1,0:T(8,128)}, f32[16,32,128]{2,1,0:T(8,128)}, f32[16,32,128]{2,1,0:T(8,128)}, f32[8,4,8,32]{3,2,1,0:T(8,128)}) custom-call(f32[4,728,128]{2,1,0:T(8,128)S(1)} %get-tuple-element.10.pad_ref, f32[4,14,16,128]{3,2,1,0:T(8,128)S(1)} %get-tuple-element.11.inner_ref, f32[6,16,32,128]{3,2,1,0:T(8,128)S(1)} %get-tuple-element.12.side_ref, ...), custom_call_target="tpu_custom_call" | custom-call | tf_op jit(solution)/shard_map/pallas_call | solution.py:631

commit v4 on v3

--- a/solution.py
+++ b/solution.py
@@ -17,6 +17,8 @@
 AHEAD = 3
 PITCH = 40
 FIRST = 8
+INNER = 14
+OUTER = 14
 
 MIX_WEIGHTS = (0.3, -0.25, 0.2, -0.15, 0.35, -0.3, 0.25, -0.2)
 RELAX_WEIGHT = 0.7
@@ -477,29 +479,32 @@
         if f == 3:
             take_eta()
 
-    def sweep(turn, first_x, end_x, first, rows):
-        def slab(x, carry):
-            moved = relax(x, first, rows, pads[turn], side_ref, rest_ref)
-            for k in range(4):
-                if turn == SWEEPS - 1:
-                    inner_ref[k, x - 1] = moved[k]
-                else:
-                    pads[turn + 1][k, pl.ds((x + 1) * PITCH + FIRST + first, rows), :] = moved[k]
+    def sweep(turn, xs, together, first, rows):
+        def slabs(step, carry):
+            for i in range(together):
+                x = xs[0] + (step * together + i) * xs[1]
+                moved = relax(x, first, rows, pads[turn], side_ref, rest_ref)
+                for k in range(4):
+                    if turn == SWEEPS - 1:
+                        inner_ref[k, x - 1] = moved[k]
+                    else:
+                        at = pl.ds((x + 1) * PITCH + FIRST + first, rows)
+                        pads[turn + 1][k, at, :] = moved[k]
             return carry
 
-        lax.fori_loop(first_x, end_x, slab, 0)
-
+        lax.fori_loop(0, xs[2] // together, slabs, 0)
+
+    inside, ends = (1, 1, nx - 2), (0, nx - 1, 2)
     for turn in range(SWEEPS):
         if turn > 0:
             send_halo(3 + turn)
-        sweep(turn, 1, nx - 1, 8, ny - 16)
+        sweep(turn, inside, INNER, 8, ny - 16)
         for group in range(4) if turn == 0 else (3 + turn,):
             take_halo(group)
         if turn < SWEEPS - 1:
-            sweep(turn, 0, 1, 0, ny)
-            sweep(turn, nx - 1, nx, 0, ny)
-            sweep(turn, 1, nx - 1, 0, 8)
-            sweep(turn, 1, nx - 1, ny - 8, 8)
+            sweep(turn, ends, 2, 0, ny)
+            for first in (0, ny - 8):
+                sweep(turn, inside, OUTER, first, 8)
 
     whole(table, table_sems.at[0], table_sems.at[1]).wait_send()
     whole(mean_land, mean_sems.at[0], mean_sems.at[1]).wait_send()
@@ -605,20 +610,22 @@
     send(inner_ref.at[pl.ds(0, 3)], velocity_ref.at[:, middle, centre])
     send(inner_ref.at[3], pressure_ref.at[middle, centre])
 
-    def sweep(first_x, end_x, first, rows):
-        def slab(x, carry):
-            moved = relax(x, first, rows, pad_ref, side_ref, rest_ref)
-            for k in range(4):
-                fresh[k, x, pl.ds(first, rows), :] = moved[k]
+    def sweep(xs, together, first, rows):
+        def slabs(step, carry):
+            for i in range(together):
+                x = xs[0] + (step * together + i) * xs[1]
+                moved = relax(x, first, rows, pad_ref, side_ref, rest_ref)
+                for k in range(4):
+                    fresh[k, x, pl.ds(first, rows), :] = moved[k]
             return carry
 
-        lax.fori_loop(first_x, end_x, slab, 0)
+        lax.fori_loop(0, xs[2] // together, slabs, 0)
 
     for first in (0, ny - 8):
-        sweep(1, nx - 1, first, 8)
+        sweep((1, 1, nx - 2), OUTER, first, 8)
         send_fresh(middle, pl.ds(first, 8))
+    sweep((0, nx - 1, 2), 2, 0, ny)
     for x in (0, nx - 1):
-        sweep(x, x + 1, 0, ny)
         send_fresh(pl.ds(x, 1), pl.ds(0, ny))
     for copy in copies:
         copy.wait()

time: 102 us -> 96.3 us (0.944)
  Pallas kernels: 102 us -> 95.5 us
    pallas_call x1, Pallas kernels: 98.3 us -> 94.2 us  [migrate(): pl.pallas_call(functools.partial(migrate_kernel, wide_count=wide_count, n...]
    pallas_call x1, Pallas kernels: 3.22 us -> 1.28 us  [last_sweep(): pl.pallas_call(last_kernel, out_shape=(jax.ShapeDtypeStruct((3, nx, ny, n...]
where the time goes in v4:
time: 96.3 us; the launch traced here: 96.1 us
  Pallas kernels  95.5 us (99%)
    pallas_call x1, Pallas kernels, migrate(): pl.pallas_call(functools.partial(migrate_kernel, wide_count=wide_count, n...  94.2 us

profile of v4, /device:TPU:1, one launch (start us, length us, event | category | flops | bytes accessed | tf_op | source)
XLA Modules:
  0.0 96.1 jit_solution(3672916052209702404)
XLA Ops:
  0.6 94.2 %shard_map.111 = (f32[4,728,128]{2,1,0:T(8,128)S(1)}, f32[4,14,16,128]{3,2,1,0:T(8,128)S(1)}, f32[6,16,32,128]{3,2,1,0:T(8,128)S(1)}, f32[3,16,32,128]{3,2,1,0:T...) custom-call(s32[16]{0:T(128)} %places_ref.1, f32[3,16,4096]{2,1,0:T(8,128)} %bitcast.3, ...), custom_call_target="tpu_custom_call" | custom-call | tf_op jit(solution)/shard_map/pallas_call | solution.py:535
  94.8 1.3 %shard_map.112 = (f32[3,16,32,128]{3,2,1,0:T(8,128)}, f32[16,32,128]{2,1,0:T(8,128)}, f32[16,32,128]{2,1,0:T(8,128)}, f32[8,4,8,32]{3,2,1,0:T(8,128)}) custom-call(f32[4,728,128]{2,1,0:T(8,128)S(1)} %get-tuple-element.10.pad_ref, f32[4,14,16,128]{3,2,1,0:T(8,128)S(1)} %get-tuple-element.11.inner_ref, f32[6,16,32,128]{3,2,1,0:T(8,128)S(1)} %get-tuple-element.12.side_ref, ...), custom_call_target="tpu_custom_call" | custom-call | tf_op jit(solution)/shard_map/pallas_call | solution.py:638

commit v5 on v3

--- a/solution.py
+++ b/solution.py
@@ -17,6 +17,9 @@
 AHEAD = 3
 PITCH = 40
 FIRST = 8
+DEEP = 3
+STEP = 16
+TOGETHER = 5
 
 MIX_WEIGHTS = (0.3, -0.25, 0.2, -0.15, 0.35, -0.3, 0.25, -0.2)
 RELAX_WEIGHT = 0.7
@@ -87,41 +90,40 @@
     )
 
 
-def factors(x, eta_ref, heat_ref, side_ref, rest_ref):
-    ny = heat_ref.shape[1]
-    base = pl.multiple_of((x + 1) * PITCH + FIRST, 8)
-    here = eta_ref[pl.ds(base, ny), :]
+def factors(base, rows, eta_ref, heat_ref, side_ref, rest_ref):
+    here = eta_ref[pl.ds(base, rows), :]
     around = [
-        eta_ref[pl.ds(base + off, ny), :] for off in (PITCH, -PITCH, 1, -1)
+        eta_ref[pl.ds(base + off, rows), :] for off in (PITCH, -PITCH, 1, -1)
     ] + list(z_pair(here))
     face = [0.5 * (here + other) for other in around]
     diagonal = face[0]
     for m in range(1, 6):
         diagonal = diagonal + face[m]
-    scale = RELAX_WEIGHT / diagonal
+    inside = here > 0.0
+    scale = jnp.where(inside, RELAX_WEIGHT / jnp.where(inside, diagonal, 1.0), 0.0)
     low_end, high_end = at_ends(here.shape)
+    own = pl.ds(base, rows)
     for m in range(6):
         value = face[m] * scale
         if m == 4:
             value = jnp.where(high_end, 0.0, value)
         elif m == 5:
             value = jnp.where(low_end, 0.0, value)
-        side_ref[m, x] = value
-    rest_ref[0, x] = 0.5 * scale
-    rest_ref[1, x] = (0.5 * PRESSURE_WEIGHT) * here
-    rest_ref[2, x] = scale * (DENSITY_FACTOR * heat_ref[x])
-
-
-def relax(x, first, rows, pad, side_ref, rest_ref):
-    base = (x + 1) * PITCH + FIRST + first
+        side_ref[m, own, :] = value
+    rest_ref[0, own, :] = 0.5 * scale
+    rest_ref[1, own, :] = (0.5 * PRESSURE_WEIGHT) * here
+    rest_ref[2, own, :] = scale * (DENSITY_FACTOR * heat_ref[own, :])
+
+
+def relax(base, rows, pad, side_ref, rest_ref):
     nz = pad.shape[2]
-    own = pl.ds(first, rows)
+    own = pl.ds(base, rows)
 
     def value(k, off=0):
         return pad[k, pl.ds(base + off, rows), :]
 
-    side = [side_ref[m, x, own, :] for m in range(6)]
-    half_scale, squeeze, lift = (rest_ref[m, x, own, :] for m in range(3))
+    side = [side_ref[m, own, :] for m in range(6)]
+    half_scale, squeeze, lift = (rest_ref[m, own, :] for m in range(3))
     press = value(3)
     press_up_z, press_down_z = z_pair(press)
     drops = (
@@ -154,13 +156,13 @@
 
 def migrate_kernel(
     places_ref, flow_ref, stress_ref, warm_ref, drag_ref, attr_ref, holder_ref, voxel_ref,
-    pad_ref, inner_ref, side_ref, rest_ref, heat_ref, mean_ref,
+    pad_ref, side_ref, rest_ref, heat_ref, mean_ref,
     slot_ref, row_ref, table, table_smem, raw, lined, mine, stage_0, stage_1, stage_2, stage_3, stage_4, stage_5,
     land_0, land_1, land_2, land_3, land_4, land_5,
     attr, holder, voxel, mean_mine, mean_stage, mean_land, mean_held, held, drag_grid,
-    pad_0, pad_1, eta, edge_in, edge_out, eta_in, eta_out,
+    eta, warm, edge_in, edge_out, corner_in, corner_out,
     raw_sems, table_sems, data_send, data_recv, mean_sems,
-    eta_send, eta_recv, halo_send, halo_recv, small_sem,
+    halo_send, halo_recv, small_sem,
     *, wide_count, narrow_count,
 ):
     count = wide_count * narrow_count
@@ -170,7 +172,6 @@
     nx, ny, nz = heat_ref.shape
     stages = (stage_0, stage_1, stage_2, stage_3, stage_4, stage_5)
     lands = (land_0, land_1, land_2, land_3, land_4, land_5)
-    pads = (pad_0, pad_1, pad_ref)
 
     to_slots = pltpu.make_async_copy(places_ref, slot_ref, small_sem)
     to_slots.start()
@@ -230,11 +231,8 @@
 
     others(send_row)
 
-    for pad in pads:
-        pad[...] = jnp.zeros(pad.shape, jnp.float32)
-    eta[...] = jnp.zeros(eta.shape, jnp.float32)
-    edge_in[...] = jnp.zeros(edge_in.shape, jnp.float32)
-    eta_in[...] = jnp.zeros(eta_in.shape, jnp.float32)
+    for ref in (pad_ref, eta, warm, edge_in, corner_in, corner_out):
+        ref[...] = jnp.zeros(ref.shape, jnp.float32)
 
     def whole(ref, send_sem, recv_sem):
         part = ref.at[pl.ds(0, count - 1)]
@@ -321,80 +319,118 @@
             held[pl.ds(z, rows, stride=LZ), :] = lands[f][source_of(y, z)]
         return swap_groups(held[...].reshape(rows, LZ, 128)).reshape(BS, BS, 128)
 
-    exists = (wide > 0, wide < wide_count - 1, narrow > 0, narrow < narrow_count - 1)
-    partner = ((wide - 1, narrow), (wide + 1, narrow), (wide, narrow - 1), (wide, narrow + 1))
-
-    def slab_rows(x):
-        return pl.ds(x * PITCH + FIRST, ny)
-
-    def edge_rows(side):
-        return pl.ds(PITCH + FIRST + (0 if side == 2 else ny - 1), nx, stride=PITCH)
-
-    def beside_rows(side):
-        return pl.ds(PITCH + FIRST + (-1 if side == 2 else ny), nx, stride=PITCH)
-
-    def eta_copy(side, arriving=False):
-        if side < 2:
-            source = eta.at[slab_rows(1 if side == 0 else nx)]
-            target = eta.at[slab_rows(nx + 1 if side == 0 else 0)]
-            mine_at = eta.at[slab_rows(0 if side == 0 else nx + 1)]
+    ways = ((-1, 0), (1, 0), (0, -1), (0, 1), (-1, -1), (-1, 1), (1, -1), (1, 1))
+    low_side = {-1: (wide > 0, narrow > 0), 1: (wide < wide_count - 1, narrow < narrow_count - 1)}
+
+    def exists(way):
+        there = [low_side[step][axis] for axis, step in enumerate(way) if step]
+        return there[0] if len(there) == 1 else there[0] & there[1]
+
+    def row_of(x, y):
+        return (x + DEEP) * PITCH + FIRST + y
+
+    def grid_rows(g, at):
+        if g < 2:
+            return (warm, eta)[g].at[at]
+        return pad_ref.at[g - 2, at]
+
+    def depth_of(g):
+        return DEEP - 1 if g == 0 else DEEP
+
+    def messages(g):
+        found = []
+        for i in range(DEEP):
+            for way, slot in ((-1, i), (1, DEEP + i)):
+                mine_x, theirs_x = (i, nx + i) if way < 0 else (nx - DEEP + i, i - DEEP)
+                here_x = i - DEEP if way < 0 else nx + i
+                rows_at = [
+                    grid_rows(g, pl.ds(row_of(x, 0), ny)) for x in (mine_x, theirs_x, here_x)
+                ]
+                found.append(
+                    ((way, 0), slot, rows_at[0], rows_at[1], (slot + DEEP) % (2 * DEEP), rows_at[2])
+                )
+        deep = pl.ds(0, depth_of(g))
+        for side, way in enumerate((-1, 1)):
+            slot = 2 * DEEP + side
+            found.append(
+                (
+                    (0, way), slot, edge_out.at[g, side, deep], edge_in.at[g, 1 - side, deep],
+                    2 * DEEP + 1 - side, edge_in.at[g, side, deep],
+                )
+            )
+        for c, way in enumerate(ways[4:]):
+            found.append(
+                (
+                    way, 2 * DEEP + 2 + c, corner_out.at[g, c], corner_in.at[g, 3 - c],
+                    2 * DEEP + 5 - c, corner_in.at[g, c],
+                )
+            )
+        return found
+
+    def each_message(g, act):
+        for way in ways:
+            group = [m for m in messages(g) if m[0] == way]
+
+            @pl.when(exists(way))
+            def _(way=way, group=group):
+                for _, slot, source, target, far_slot, here in group:
+                    act(way, slot, source, target, far_slot, here)
+
+    def start_message(g):
+        def act(way, slot, source, target, far_slot, here):
+            pltpu.make_async_remote_copy(
+                src_ref=source, dst_ref=target,
+                send_sem=halo_send.at[g, slot], recv_sem=halo_recv.at[g, far_slot],
+                device_id=(wide + way[0], narrow + way[1]), device_id_type=MESH,
+            ).start()
+
+        return act
+
+    def wait_message(g, sent):
+        def act(way, slot, source, target, far_slot, here):
+            copy = pltpu.make_async_remote_copy(
+                src_ref=source if sent else here, dst_ref=target if sent else here,
+                send_sem=halo_send.at[g, slot], recv_sem=halo_recv.at[g, slot],
+                device_id=(wide + way[0], narrow + way[1]), device_id_type=MESH,
+            )
+            copy.wait_send() if sent else copy.wait_recv()
+
+        return act
+
+    def read_rows(g, at):
+        return (warm, eta)[g][at, :] if g < 2 else pad_ref[g - 2, at, :]
+
+    def write_rows(g, at, value):
+        if g < 2:
+            (warm, eta)[g][at, :] = value
         else:
-            source = eta_out.at[side - 2]
-            target = eta_in.at[3 - side]
-            mine_at = eta_in.at[side - 2]
-        return pltpu.make_async_remote_copy(
-            src_ref=mine_at if arriving else source,
-            dst_ref=mine_at if arriving else target,
-            send_sem=eta_send.at[side],
-            recv_sem=eta_recv.at[side if arriving else side ^ 1],
-            device_id=partner[side],
-            device_id_type=MESH,
-        )
-
-    groups = ((0, 0, 1), (0, 1, 1), (0, 2, 1), (0, 3, 1), (1, 0, 4), (2, 0, 4))
-
-    def halo_copy(group, side, arriving=False):
-        turn, first, fields = groups[group]
-        ks = pl.ds(first, fields)
-        pad = pads[turn]
-        if side < 2:
-            source = pad.at[ks, slab_rows(1 if side == 0 else nx)]
-            target = pad.at[ks, slab_rows(nx + 1 if side == 0 else 0)]
-            mine_at = pad.at[ks, slab_rows(0 if side == 0 else nx + 1)]
-        else:
-            source = edge_out.at[turn, side - 2, ks]
-            target = edge_in.at[turn, 3 - side, ks]
-            mine_at = edge_in.at[turn, side - 2, ks]
-        return pltpu.make_async_remote_copy(
-            src_ref=mine_at if arriving else source,
-            dst_ref=mine_at if arriving else target,
-            send_sem=halo_send.at[group, side],
-            recv_sem=halo_recv.at[group, side if arriving else side ^ 1],
-            device_id=partner[side],
-            device_id_type=MESH,
-        )
-
-    def each_side(act, sides=range(4)):
-        for side in sides:
-
-            @pl.when(exists[side])
-            def _(side=side):
-                act(side)
-
-    def send_halo(group):
-        turn, first, fields = groups[group]
-        each_side(lambda side: halo_copy(group, side).start(), range(2))
-        for k in range(first, first + fields):
-            for side in (2, 3):
-                edge_out[turn, side - 2, k] = pads[turn][k, edge_rows(side), :]
-        each_side(lambda side: halo_copy(group, side).start(), range(2, 4))
-
-    def take_halo(group):
-        turn, first, fields = groups[group]
-        each_side(lambda side: halo_copy(group, side, True).wait_recv())
-        for k in range(first, first + fields):
-            for side in (2, 3):
-                pads[turn][k, beside_rows(side), :] = edge_in[turn, side - 2, k]
+            pad_ref[g - 2, at, :] = value
+
+    def send_halo(g):
+        depth = depth_of(g)
+        for side in range(2):
+            for i in range(depth):
+                y = i if side == 0 else ny - depth + i
+                edge_out[g, side, i] = read_rows(g, pl.ds(row_of(0, y), nx, stride=PITCH))
+        for c, (dx, dy) in enumerate(ways[4:]):
+            for i in range(2):
+                x = i if dx < 0 else nx - 2 + i
+                y = 0 if dy < 0 else ny - 2
+                corner_out[g, c, 2 * i : 2 * i + 2, :] = read_rows(g, pl.ds(row_of(x, y), 2))
+        each_message(g, start_message(g))
+
+    def take_halo(g):
+        depth = depth_of(g)
+        each_message(g, wait_message(g, False))
+        for side in range(2):
+            for i in range(depth):
+                y = i - depth if side == 0 else ny + i
+                write_rows(g, pl.ds(row_of(0, y), nx, stride=PITCH), edge_in[g, side, i])
+        for c, (dx, dy) in enumerate(ways[4:]):
+            for i in range(2):
+                x = i - 2 if dx < 0 else nx + i
+                y = -2 if dy < 0 else ny
+                write_rows(g, pl.ds(row_of(x, y), 2), corner_in[g, c, 2 * i : 2 * i + 2, :])
 
     def viscosity():
         whole(mean_land, mean_sems.at[0], mean_sems.at[1]).wait_recv()
@@ -438,23 +474,19 @@
                 [jnp.broadcast_to(wide_mix[j : j + 1], (4, 128)) for j in range(LY * 4)], axis=0
             )
             for x in range(layer * 4, layer * 4 + 4):
-                eta[slab_rows(x + 1), :] = drag_grid[x] * jnp.exp(
+                eta[pl.ds(row_of(x, 0), ny), :] = drag_grid[x] * jnp.exp(
                     HEAT_FACTOR * (0.5 - heat_ref[x]) + spread
                 )
-        for side in (2, 3):
-            eta_out[side - 2] = eta[edge_rows(side), :]
-        each_side(lambda side: eta_copy(side).start())
-
-    def take_eta():
-        each_side(lambda side: eta_copy(side, True).wait_recv())
-        for side in (2, 3):
-            eta[beside_rows(side), :] = eta_in[side - 2]
-
-        def slab(x, carry):
-            factors(x, eta, heat_ref, side_ref, rest_ref)
+
+    def all_factors():
+        step_rows = STEP * TOGETHER
+
+        def step(turn, carry):
+            base = pl.multiple_of(PITCH + turn * step_rows, 8)
+            factors(base, step_rows, eta, warm, side_ref, rest_ref)
             return carry
 
-        lax.fori_loop(0, nx, slab, 0)
+        lax.fori_loop(0, (nx + 2 * DEEP - 2) * PITCH // step_rows, step, 0)
 
     for f in range(FIELDS):
         whole(lands[f], data_send.at[f], data_recv.at[f]).wait_recv()
@@ -465,49 +497,27 @@
             part = grid_part(f, y)
             if f == 0:
                 heat_ref[:, at, :] = part
-            elif f == 1:
+            if f == 1:
                 drag_grid[:, at, :] = part
             else:
                 for x in range(nx):
-                    pad_0[f - 2, pl.ds((x + 1) * PITCH + FIRST + y * BS, BS), :] = part[x]
+                    write_rows(f, pl.ds(row_of(x, y * BS), BS), part[x])
         if f == 1:
             viscosity()
-        elif f > 1:
-            send_halo(f - 2)
+        send_halo(f)
         if f == 3:
-            take_eta()
-
-    def sweep(turn, first_x, end_x, first, rows):
-        def slab(x, carry):
-            moved = relax(x, first, rows, pads[turn], side_ref, rest_ref)
-            for k in range(4):
-                if turn == SWEEPS - 1:
-                    inner_ref[k, x - 1] = moved[k]
-                else:
-                    pads[turn + 1][k, pl.ds((x + 1) * PITCH + FIRST + first, rows), :] = moved[k]
-            return carry
-
-        lax.fori_loop(first_x, end_x, slab, 0)
-
-    for turn in range(SWEEPS):
-        if turn > 0:
-            send_halo(3 + turn)
-        sweep(turn, 1, nx - 1, 8, ny - 16)
-        for group in range(4) if turn == 0 else (3 + turn,):
-            take_halo(group)
-        if turn < SWEEPS - 1:
-            sweep(turn, 0, 1, 0, ny)
-            sweep(turn, nx - 1, nx, 0, ny)
-            sweep(turn, 1, nx - 1, 0, 8)
-            sweep(turn, 1, nx - 1, ny - 8, 8)
+            take_halo(0)
+            take_halo(1)
+            all_factors()
+    for f in range(2, FIELDS):
+        take_halo(f)
 
     whole(table, table_sems.at[0], table_sems.at[1]).wait_send()
     whole(mean_land, mean_sems.at[0], mean_sems.at[1]).wait_send()
     for f in range(FIELDS):
         whole(lands[f], data_send.at[f], data_recv.at[f]).wait_send()
-    each_side(lambda side: eta_copy(side).wait_send())
-    for group in range(len(groups)):
-        each_side(lambda side: halo_copy(group, side).wait_send())
+    for f in range(FIELDS):
+        each_message(f, wait_message(f, True))
 
 
 def migrate(slots, flow, stress, heat, drag, attributes, holder, voxel):
@@ -517,7 +527,7 @@
     tracers = attributes.shape[1]
     nx, ny, nz = LX * BS, LY * BS, LZ * BS
     rows = BS * BS * BS // 128
-    pad_rows = (nx + 2) * PITCH + 8
+    pad_rows = (nx + 2 * DEEP) * PITCH + 8
     vmem = pl.BlockSpec(memory_space=pltpu.VMEM)
     hbm = pl.BlockSpec(memory_space=pltpu.HBM)
     f32 = jnp.float32
@@ -531,14 +541,13 @@
         functools.partial(migrate_kernel, wide_count=wide_count, narrow_count=narrow_count),
         out_shape=(
             jax.ShapeDtypeStruct((4, pad_rows, nz), f32),
-            jax.ShapeDtypeStruct((4, nx - 2, ny - 16, nz), f32),
-            jax.ShapeDtypeStruct((6, nx, ny, nz), f32),
-            jax.ShapeDtypeStruct((3, nx, ny, nz), f32),
+            jax.ShapeDtypeStruct((6, pad_rows, nz), f32),
+            jax.ShapeDtypeStruct((3, pad_rows, nz), f32),
             jax.ShapeDtypeStruct((nx, ny, nz), f32),
             jax.ShapeDtypeStruct((8, LX * 4, LY * 4, LZ * 4), f32),
         ),
         in_specs=[hbm] * 8,
-        out_specs=(vmem,) * 6,
+        out_specs=(vmem,) * 5,
         scratch_shapes=[
             pltpu.SMEM((blocks,), jnp.int32),
             pltpu.VMEM((1, 128), jnp.int32),
@@ -558,35 +567,32 @@
             pltpu.VMEM((4 * LZ, 128), f32),
             pltpu.VMEM((rows * LZ, 128), f32),
             pltpu.VMEM((nx, ny, nz), f32),
-            pltpu.VMEM((4, pad_rows, nz), f32),
-            pltpu.VMEM((4, pad_rows, nz), f32),
             pltpu.VMEM((pad_rows, nz), f32),
-            pltpu.VMEM((SWEEPS, 2, 4, nx, nz), f32),
-            pltpu.VMEM((SWEEPS, 2, 4, nx, nz), f32),
-            pltpu.VMEM((2, nx, nz), f32),
-            pltpu.VMEM((2, nx, nz), f32),
+            pltpu.VMEM((pad_rows, nz), f32),
+            pltpu.VMEM((FIELDS, 2, DEEP, nx, nz), f32),
+            pltpu.VMEM((FIELDS, 2, DEEP, nx, nz), f32),
+            pltpu.VMEM((FIELDS, 4, 8, nz), f32),
+            pltpu.VMEM((FIELDS, 4, 8, nz), f32),
             dma((FIELDS + 3,)),
             dma((2,)),
             dma((FIELDS,)),
             dma((FIELDS,)),
             dma((2,)),
-            dma((4,)),
-            dma((4,)),
-            dma((SWEEPS + 3, 4)),
-            dma((SWEEPS + 3, 4)),
+            dma((FIELDS, 2 * DEEP + 6)),
+            dma((FIELDS, 2 * DEEP + 6)),
             dma(()),
         ],
         compiler_params=pltpu.CompilerParams(
             collective_id=1,
             has_side_effects=True,
-            vmem_limit_bytes=(24 if count <= 32 else 52) * 1024 * 1024,
+            vmem_limit_bytes=(24 if count <= 32 else 44) * 1024 * 1024,
         ),
     )(*pinned)
 
 
-def last_kernel(
-    pad_ref, inner_ref, side_ref, rest_ref, heat_ref, mean_ref,
-    velocity_ref, pressure_ref, heat_out_ref, mean_out_ref, fresh, sems,
+def relax_kernel(
+    pad_ref, side_ref, rest_ref, heat_ref, mean_ref,
+    velocity_ref, pressure_ref, heat_out_ref, mean_out_ref, pad_1, pad_2, fresh, sems,
 ):
     nx, ny, nz = heat_ref.shape
     copies = []
@@ -595,55 +601,67 @@
         copies.append(pltpu.make_async_copy(source, target, sems.at[len(copies)]))
         copies[-1].start()
 
-    def send_fresh(xs, ys):
-        send(fresh.at[pl.ds(0, 3), xs, ys], velocity_ref.at[:, xs, ys])
-        send(fresh.at[3, xs, ys], pressure_ref.at[xs, ys])
-
     send(heat_ref, heat_out_ref)
     send(mean_ref, mean_out_ref)
-    middle, centre = pl.ds(1, nx - 2), pl.ds(8, ny - 16)
-    send(inner_ref.at[pl.ds(0, 3)], velocity_ref.at[:, middle, centre])
-    send(inner_ref.at[3], pressure_ref.at[middle, centre])
-
-    def sweep(first_x, end_x, first, rows):
-        def slab(x, carry):
-            moved = relax(x, first, rows, pad_ref, side_ref, rest_ref)
-            for k in range(4):
-                fresh[k, x, pl.ds(first, rows), :] = moved[k]
+
+    for turn, (old, new) in enumerate(((pad_ref, pad_1), (pad_1, pad_2))):
+        first = turn + 1
+        slabs = nx + 2 * DEEP - 2 * first
+
+        def rows_on(step, carry, first=first, old=old, new=new):
+            for i in range(TOGETHER):
+                base = pl.multiple_of(first * PITCH + (step * TOGETHER + i) * STEP, 8)
+                moved = relax(base, STEP, old, side_ref, rest_ref)
+                for k in range(4):
+                    new[k, pl.ds(base, STEP), :] = moved[k]
             return carry
 
-        lax.fori_loop(first_x, end_x, slab, 0)
-
-    for first in (0, ny - 8):
-        sweep(1, nx - 1, first, 8)
-        send_fresh(middle, pl.ds(first, 8))
-    for x in (0, nx - 1):
-        sweep(x, x + 1, 0, ny)
-        send_fresh(pl.ds(x, 1), pl.ds(0, ny))
+        lax.fori_loop(0, slabs * PITCH // (STEP * TOGETHER), rows_on, 0)
+
+    parts = 4
+    thick = nx // parts
+    for part in range(parts):
+
+        def slabs_on(step, carry):
+            for i in range(2):
+                x = part * thick + step * 2 + i
+                for half in range(ny // STEP):
+                    base = pl.multiple_of((x + DEEP) * PITCH + FIRST + half * STEP, 8)
+                    moved = relax(base, STEP, pad_2, side_ref, rest_ref)
+                    for k in range(4):
+                        fresh[k, x, half * STEP : (half + 1) * STEP, :] = moved[k]
+            return carry
+
+        lax.fori_loop(0, thick // 2, slabs_on, 0)
+        at = pl.ds(part * thick, thick)
+        send(fresh.at[pl.ds(0, 3), at], velocity_ref.at[:, at])
+        send(fresh.at[3, at], pressure_ref.at[at])
     for copy in copies:
         copy.wait()
 
 
-def last_sweep(pad, inner, side, rest, heat, means):
+def relax_all(pad, side, rest, heat, means):
     nx, ny, nz = heat.shape
     vmem = pl.BlockSpec(memory_space=pltpu.VMEM)
     hbm = pl.BlockSpec(memory_space=pltpu.HBM)
     return pl.pallas_call(
-        last_kernel,
+        relax_kernel,
         out_shape=(
             jax.ShapeDtypeStruct((3, nx, ny, nz), jnp.float32),
             jax.ShapeDtypeStruct((nx, ny, nz), jnp.float32),
             jax.ShapeDtypeStruct(heat.shape, jnp.float32),
             jax.ShapeDtypeStruct(means.shape, jnp.float32),
         ),
-        in_specs=[vmem] * 6,
+        in_specs=[vmem] * 5,
         out_specs=(hbm,) * 4,
         scratch_shapes=[
+            pltpu.VMEM(pad.shape, jnp.float32),
+            pltpu.VMEM(pad.shape, jnp.float32),
             pltpu.VMEM((4, nx, ny, nz), jnp.float32),
-            pltpu.SemaphoreType.DMA((12,)),
+            pltpu.SemaphoreType.DMA((10,)),
         ],
         compiler_params=pltpu.CompilerParams(vmem_limit_bytes=16 * 1024 * 1024),
-    )(pad, inner, side, rest, heat, means)
+    )(pad, side, rest, heat, means)
 
 
 def per_device(
@@ -667,7 +685,7 @@
         marker_holding_tile.reshape(1, tracers),
         marker_voxel_number.reshape(1, tracers),
     )
-    return last_sweep(*results)
+    return relax_all(*results)
 
 
 def solution(mesh):

time: 102 us -> 95.3 us (0.934)
  Pallas kernels: 102 us -> 94.5 us
    pallas_call x1, Pallas kernels: 98.3 us -> 89.4 us  [migrate(): pl.pallas_call(functools.partial(migrate_kernel, wide_count=wide_count, n...]
    pallas_call x1, Pallas kernels: 3.22 us -> 5.08 us  [relax_all(): pl.pallas_call(relax_kernel, out_shape=(jax.ShapeDtypeStruct((3, nx, ny,...]
where the time goes in v5:
time: 95.3 us; the launch traced here: 95.1 us
  Pallas kernels  94.5 us (99%)
    pallas_call x1, Pallas kernels, migrate(): pl.pallas_call(functools.partial(migrate_kernel, wide_count=wide_count, n...  89.4 us
    pallas_call x1, Pallas kernels, relax_all(): pl.pallas_call(relax_kernel, out_shape=(jax.ShapeDtypeStruct((3, nx, ny,...  5.08 us

profile of v5, /device:TPU:1, one launch (start us, length us, event | category | flops | bytes accessed | tf_op | source)
XLA Modules:
  0.0 95.1 jit_solution(2951316835460142970)
XLA Ops:
  0.6 89.4 %shard_map.111 = (f32[4,888,128]{2,1,0:T(8,128)S(1)}, f32[6,888,128]{2,1,0:T(8,128)S(1)}, f32[3,888,128]{2,1,0:T(8,128)S(1)}, f32[16,32,128]{2,1,0:T(8,128)S(1)}, f32[8,4,8,32]{3,2,1,0:T(8,128)S(1)}) custom-call(s32[16]{0:T(128)} %places_ref.1, f32[3,16,4096]{2,1,0:T(8,128)} %bitcast.3, f32[16,4096]{1,0:T(8,128)} %stress_ref.1, f32[16,4096]{1,0:T(8,128)} %warm_ref.1, ...), custom_call_target="tpu_custom_call" | custom-call | tf_op jit(solution)/shard_map/pallas_call | solution.py:540
  90.0 5.1 %shard_map.112 = (f32[3,16,32,128]{3,2,1,0:T(8,128)}, f32[16,32,128]{2,1,0:T(8,128)}, f32[16,32,128]{2,1,0:T(8,128)}, f32[8,4,8,32]{3,2,1,0:T(8,128)}) custom-call(f32[4,888,128]{2,1,0:T(8,128)S(1)} %get-tuple-element.9.pad_ref, f32[6,888,128]{2,1,0:T(8,128)S(1)} %get-tuple-element.10.side_ref, f32[3,888,128]{2,1,0:T(8,128)S(1)} %get-tuple-element.11.rest_ref, ...), custom_call_target="tpu_custom_call" | custom-call | tf_op jit(solution)/shard_map/pallas_call | solution.py:647

commit v6 on v5

--- a/solution.py
+++ b/solution.py
@@ -19,7 +19,8 @@
 FIRST = 8
 DEEP = 3
 STEP = 16
-TOGETHER = 5
+TURNS = 1
+DRIFT_TURNS = 5
 
 MIX_WEIGHTS = (0.3, -0.25, 0.2, -0.15, 0.35, -0.3, 0.25, -0.2)
 RELAX_WEIGHT = 0.7
@@ -115,7 +116,7 @@
     rest_ref[2, own, :] = scale * (DENSITY_FACTOR * heat_ref[own, :])
 
 
-def relax(base, rows, pad, side_ref, rest_ref):
+def drift(base, rows, pad, side_ref, rest_ref):
     nz = pad.shape[2]
     own = pl.ds(base, rows)
 
@@ -123,15 +124,7 @@
         return pad[k, pl.ds(base + off, rows), :]
 
     side = [side_ref[m, own, :] for m in range(6)]
-    half_scale, squeeze, lift = (rest_ref[m, own, :] for m in range(3))
-    press = value(3)
-    press_up_z, press_down_z = z_pair(press)
-    drops = (
-        value(3, PITCH) - value(3, -PITCH),
-        value(3, 1) - value(3, -1),
-        press_up_z - press_down_z,
-    )
-    moved = []
+    found = []
     divergence = None
     for k in range(3):
         here = value(k)
@@ -142,21 +135,50 @@
         near = (
             value(k, PITCH), value(k, -PITCH), value(k, 1), value(k, -1), up_z, down_z,
         )
-        fresh = (1.0 - RELAX_WEIGHT) * here - half_scale * drops[k]
+        fresh = (1.0 - RELAX_WEIGHT) * here
         for m in range(6):
             fresh = fresh + side[m] * near[m]
         if k == 2:
-            fresh = fresh + lift
-        moved.append(fresh)
+            fresh = fresh + rest_ref[2, own, :]
+        found.append(fresh)
         flux = near[2 * k] - near[2 * k + 1]
         divergence = flux if divergence is None else divergence + flux
-    moved.append(press - squeeze * divergence)
-    return moved
+    found.append(rest_ref[1, own, :] * divergence)
+    return found
+
+
+def push(base, rows, pad, rest_ref, drifted):
+    own = pl.ds(base, rows)
+
+    def value(off=0):
+        return pad[3, pl.ds(base + off, rows), :]
+
+    press = value()
+    up_z, down_z = z_pair(press)
+    half_scale = rest_ref[0, own, :]
+    drops = (value(PITCH) - value(-PITCH), value(1) - value(-1), up_z - down_z)
+    return [drifted[k] - half_scale * drops[k] for k in range(3)] + [press - drifted[3]]
+
+
+def relax(base, rows, pad, side_ref, rest_ref):
+    return push(base, rows, pad, rest_ref, drift(base, rows, pad, side_ref, rest_ref))
+
+
+def over_rows(first, last, turns, act):
+    together = (last - first) // (STEP * turns)
+    assert together * STEP * turns == last - first
+
+    def step(turn, carry):
+        for i in range(together):
+            act(pl.multiple_of(first + (turn * together + i) * STEP, 8))
+        return carry
+
+    lax.fori_loop(0, turns, step, 0)
 
 
 def migrate_kernel(
     places_ref, flow_ref, stress_ref, warm_ref, drag_ref, attr_ref, holder_ref, voxel_ref,
-    pad_ref, side_ref, rest_ref, heat_ref, mean_ref,
+    pad_ref, part_ref, side_ref, rest_ref, heat_ref, mean_ref,
     slot_ref, row_ref, table, table_smem, raw, lined, mine, stage_0, stage_1, stage_2, stage_3, stage_4, stage_5,
     land_0, land_1, land_2, land_3, land_4, land_5,
     attr, holder, voxel, mean_mine, mean_stage, mean_land, mean_held, held, drag_grid,
@@ -187,18 +209,25 @@
     for load in loads:
         load.start()
 
+    def flipped(k):
+        place, bit = narrow, 1
+        while bit < narrow_count:
+            if k & bit:
+                place = place + bit * (1 - 2 * lax.rem(lax.div(narrow, bit), 2))
+            bit *= 2
+        return place
+
+    far_first = [*range(narrow_count // 2, narrow_count), *range(1, narrow_count // 2), 0]
+
     def others(act):
-        near = [lax.rem(narrow + b, narrow_count) for b in range(narrow_count)]
-        for b in range(1, narrow_count):
-            act(wide, near[b])
-
-        def row(a, carry):
-            far = lax.rem(wide + a, wide_count)
-            for b in range(narrow_count):
-                act(far, near[b])
-            return carry
-
-        lax.fori_loop(1, wide_count, row, 0)
+        for k in far_first:
+            near = flipped(k)
+
+            def step(a, carry, near=near):
+                act(lax.rem(wide + a, wide_count), near)
+                return carry
+
+            lax.fori_loop(0 if k else 1, wide_count, step, 0)
 
     barrier = pltpu.get_barrier_semaphore()
     others(
@@ -478,15 +507,15 @@
                     HEAT_FACTOR * (0.5 - heat_ref[x]) + spread
                 )
 
-    def all_factors():
-        step_rows = STEP * TOGETHER
-
-        def step(turn, carry):
-            base = pl.multiple_of(PITCH + turn * step_rows, 8)
-            factors(base, step_rows, eta, warm, side_ref, rest_ref)
-            return carry
-
-        lax.fori_loop(0, (nx + 2 * DEEP - 2) * PITCH // step_rows, step, 0)
+    wide_rows = (PITCH, (nx + 2 * DEEP - 1) * PITCH)
+
+    def factor_rows(base):
+        factors(base, STEP, eta, warm, side_ref, rest_ref)
+
+    def drift_rows(base):
+        found = drift(base, STEP, pad_ref, side_ref, rest_ref)
+        for k in range(4):
+            part_ref[k, pl.ds(base, STEP), :] = found[k]
 
     for f in range(FIELDS):
         whole(lands[f], data_send.at[f], data_recv.at[f]).wait_recv()
@@ -508,9 +537,11 @@
         if f == 3:
             take_halo(0)
             take_halo(1)
-            all_factors()
-    for f in range(2, FIELDS):
+            over_rows(*wide_rows, 10, factor_rows)
+    for f in range(2, FIELDS - 1):
         take_halo(f)
+    over_rows(*wide_rows, DRIFT_TURNS, drift_rows)
+    take_halo(FIELDS - 1)
 
     whole(table, table_sems.at[0], table_sems.at[1]).wait_send()
     whole(mean_land, mean_sems.at[0], mean_sems.at[1]).wait_send()
@@ -541,13 +572,14 @@
         functools.partial(migrate_kernel, wide_count=wide_count, narrow_count=narrow_count),
         out_shape=(
             jax.ShapeDtypeStruct((4, pad_rows, nz), f32),
+            jax.ShapeDtypeStruct((4, pad_rows, nz), f32),
             jax.ShapeDtypeStruct((6, pad_rows, nz), f32),
             jax.ShapeDtypeStruct((3, pad_rows, nz), f32),
             jax.ShapeDtypeStruct((nx, ny, nz), f32),
             jax.ShapeDtypeStruct((8, LX * 4, LY * 4, LZ * 4), f32),
         ),
         in_specs=[hbm] * 8,
-        out_specs=(vmem,) * 5,
+        out_specs=(vmem,) * 6,
         scratch_shapes=[
             pltpu.SMEM((blocks,), jnp.int32),
             pltpu.VMEM((1, 128), jnp.int32),
@@ -591,7 +623,7 @@
 
 
 def relax_kernel(
-    pad_ref, side_ref, rest_ref, heat_ref, mean_ref,
+    pad_ref, part_ref, side_ref, rest_ref, heat_ref, mean_ref,
     velocity_ref, pressure_ref, heat_out_ref, mean_out_ref, pad_1, pad_2, fresh, sems,
 ):
     nx, ny, nz = heat_ref.shape
@@ -604,35 +636,30 @@
     send(heat_ref, heat_out_ref)
     send(mean_ref, mean_out_ref)
 
-    for turn, (old, new) in enumerate(((pad_ref, pad_1), (pad_1, pad_2))):
-        first = turn + 1
-        slabs = nx + 2 * DEEP - 2 * first
-
-        def rows_on(step, carry, first=first, old=old, new=new):
-            for i in range(TOGETHER):
-                base = pl.multiple_of(first * PITCH + (step * TOGETHER + i) * STEP, 8)
-                moved = relax(base, STEP, old, side_ref, rest_ref)
-                for k in range(4):
-                    new[k, pl.ds(base, STEP), :] = moved[k]
-            return carry
-
-        lax.fori_loop(0, slabs * PITCH // (STEP * TOGETHER), rows_on, 0)
+    def finish_first(base):
+        drifted = [part_ref[k, pl.ds(base, STEP), :] for k in range(4)]
+        moved = push(base, STEP, pad_ref, rest_ref, drifted)
+        for k in range(4):
+            pad_1[k, pl.ds(base, STEP), :] = moved[k]
+
+    def second(base):
+        moved = relax(base, STEP, pad_1, side_ref, rest_ref)
+        for k in range(4):
+            pad_2[k, pl.ds(base, STEP), :] = moved[k]
+
+    slabs = nx + 2 * DEEP
+    over_rows(PITCH, (slabs - 1) * PITCH, TURNS, finish_first)
+    over_rows(2 * PITCH, (slabs - 2) * PITCH, TURNS, second)
 
     parts = 4
     thick = nx // parts
     for part in range(parts):
-
-        def slabs_on(step, carry):
-            for i in range(2):
-                x = part * thick + step * 2 + i
-                for half in range(ny // STEP):
-                    base = pl.multiple_of((x + DEEP) * PITCH + FIRST + half * STEP, 8)
-                    moved = relax(base, STEP, pad_2, side_ref, rest_ref)
-                    for k in range(4):
-                        fresh[k, x, half * STEP : (half + 1) * STEP, :] = moved[k]
-            return carry
-
-        lax.fori_loop(0, thick // 2, slabs_on, 0)
+        for x in range(part * thick, (part + 1) * thick):
+            for half in range(0, ny, STEP):
+                base = (x + DEEP) * PITCH + FIRST + half
+                moved = relax(base, STEP, pad_2, side_ref, rest_ref)
+                for k in range(4):
+                    fresh[k, x, half : half + STEP, :] = moved[k]
         at = pl.ds(part * thick, thick)
         send(fresh.at[pl.ds(0, 3), at], velocity_ref.at[:, at])
         send(fresh.at[3, at], pressure_ref.at[at])
@@ -640,7 +667,7 @@
         copy.wait()
 
 
-def relax_all(pad, side, rest, heat, means):
+def relax_all(pad, part, side, rest, heat, means):
     nx, ny, nz = heat.shape
     vmem = pl.BlockSpec(memory_space=pltpu.VMEM)
     hbm = pl.BlockSpec(memory_space=pltpu.HBM)
@@ -652,7 +679,7 @@
             jax.ShapeDtypeStruct(heat.shape, jnp.float32),
             jax.ShapeDtypeStruct(means.shape, jnp.float32),
         ),
-        in_specs=[vmem] * 5,
+        in_specs=[vmem] * 6,
         out_specs=(hbm,) * 4,
         scratch_shapes=[
             pltpu.VMEM(pad.shape, jnp.float32),
@@ -661,7 +688,7 @@
             pltpu.SemaphoreType.DMA((10,)),
         ],
         compiler_params=pltpu.CompilerParams(vmem_limit_bytes=16 * 1024 * 1024),
-    )(pad, side, rest, heat, means)
+    )(pad, part, side, rest, heat, means)
 
 
 def per_device(

time: 95.3 us -> 93 us (0.976)
  Pallas kernels: 94.5 us -> 92.2 us
    pallas_call x1, Pallas kernels: 5.08 us -> 2.54 us  [relax_all(): pl.pallas_call(relax_kernel, out_shape=(jax.ShapeDtypeStruct((3, nx, ny,...]
where the time goes in v6:
time: 93 us; the launch traced here: 92.8 us
  Pallas kernels  92.2 us (99%)
    pallas_call x1, Pallas kernels, migrate(): pl.pallas_call(functools.partial(migrate_kernel, wide_count=wide_count, n...  89.6 us
    pallas_call x1, Pallas kernels, relax_all(): pl.pallas_call(relax_kernel, out_shape=(jax.ShapeDtypeStruct((3, nx, ny,...  2.54 us

profile of v6, /device:TPU:1, one launch (start us, length us, event | category | flops | bytes accessed | tf_op | source)
XLA Modules:
  0.0 92.8 jit_solution(4589592883612035760)
XLA Ops:
  0.6 89.6 %shard_map.111 = (f32[4,888,128]{2,1,0:T(8,128)S(1)}, f32[4,888,128]{2,1,0:T(8,128)S(1)}, f32[6,888,128]{2,1,0:T(8,128)S(1)}, f32[3,888,128]{2,1,0:T(8,128)S(1)}...) custom-call(s32[16]{0:T(128)} %places_ref.1, f32[3,16,4096]{2,1,0:T(8,128)} %bitcast.3, f32[16,4096]{1,0:T(8,128)} %stress_ref.1, ...), custom_call_target="tpu_custom_call" | custom-call | tf_op jit(solution)/shard_map/pallas_call | solution.py:571
  90.3 2.5 %shard_map.112 = (f32[3,16,32,128]{3,2,1,0:T(8,128)}, f32[16,32,128]{2,1,0:T(8,128)}, f32[16,32,128]{2,1,0:T(8,128)}, f32[8,4,8,32]{3,2,1,0:T(8,128)}) custom-call(f32[4,888,128]{2,1,0:T(8,128)S(1)} %get-tuple-element.10.pad_ref, f32[4,888,128]{2,1,0:T(8,128)S(1)} %get-tuple-element.11.part_ref, f32[6,888,128]{2,1,0:T(8,128)S(1)} %get-tuple-element.12.side_ref, ...), custom_call_target="tpu_custom_call" | custom-call | tf_op jit(solution)/shard_map/pallas_call | solution.py:674

commit v7 on v6

--- a/solution.py
+++ b/solution.py
@@ -183,7 +183,7 @@
     land_0, land_1, land_2, land_3, land_4, land_5,
     attr, holder, voxel, mean_mine, mean_stage, mean_land, mean_held, held, drag_grid,
     eta, warm, edge_in, edge_out, corner_in, corner_out,
-    raw_sems, table_sems, data_send, data_recv, mean_sems,
+    raw_sems, table_send, table_recv, data_send, data_recv, mean_sems,
     halo_send, halo_recv, small_sem,
     *, wide_count, narrow_count,
 ):
@@ -197,6 +197,39 @@
 
     to_slots = pltpu.make_async_copy(places_ref, slot_ref, small_sem)
     to_slots.start()
+    def flipped(k):
+        place, bit = narrow, 1
+        while bit < narrow_count:
+            if k & bit:
+                place = place + bit * (1 - 2 * lax.rem(lax.div(narrow, bit), 2))
+            bit *= 2
+        return place
+
+    middle = narrow_count // 2
+    upper = lax.div(narrow, middle)
+    across = [(middle + i) * (1 - upper) + (middle - 1 - i) * upper for i in range(middle)]
+    planes = across + [flipped(k) for k in range(1, middle)] + [narrow]
+    farthest_first = across[::-1] + planes[middle:]
+
+    def to_plane(plane, act):
+        def step(a, carry):
+            act(lax.rem(wide + a, wide_count), plane)
+            return carry
+
+        lax.fori_loop(1 if plane is narrow else 0, wide_count, step, 0)
+
+    def others(act, order=planes):
+        for plane in order:
+            to_plane(plane, act)
+
+    barrier = pltpu.get_barrier_semaphore()
+    others(
+        lambda w, n: pl.semaphore_signal(
+            barrier, inc=1, device_id=(w, n), device_id_type=MESH
+        ),
+        farthest_first,
+    )
+
     sources = (
         warm_ref, drag_ref, flow_ref.at[0], flow_ref.at[1], flow_ref.at[2], stress_ref,
     )
@@ -209,32 +242,6 @@
     for load in loads:
         load.start()
 
-    def flipped(k):
-        place, bit = narrow, 1
-        while bit < narrow_count:
-            if k & bit:
-                place = place + bit * (1 - 2 * lax.rem(lax.div(narrow, bit), 2))
-            bit *= 2
-        return place
-
-    far_first = [*range(narrow_count // 2, narrow_count), *range(1, narrow_count // 2), 0]
-
-    def others(act):
-        for k in far_first:
-            near = flipped(k)
-
-            def step(a, carry, near=near):
-                act(lax.rem(wide + a, wide_count), near)
-                return carry
-
-            lax.fori_loop(0 if k else 1, wide_count, step, 0)
-
-    barrier = pltpu.get_barrier_semaphore()
-    others(
-        lambda w, n: pl.semaphore_signal(
-            barrier, inc=1, device_id=(w, n), device_id_type=MESH
-        )
-    )
     to_slots.wait()
     lane = lax.broadcasted_iota(jnp.int32, (1, 128), 1)
     places = jnp.zeros((1, 128), jnp.int32)
@@ -245,15 +252,15 @@
         places = jnp.where(lane == owner, local, places)
         my_own = jnp.where(owner == me, local, my_own)
     row_ref[...] = places
-    table[me] = places
+    table[narrow * wide_count + wide] = places
     pl.semaphore_wait(barrier, count - 1)
 
     def send_row(w, n):
         pltpu.make_async_remote_copy(
             src_ref=row_ref,
-            dst_ref=table.at[me],
-            send_sem=table_sems.at[0],
-            recv_sem=table_sems.at[1],
+            dst_ref=table.at[narrow * wide_count + wide],
+            send_sem=table_send,
+            recv_sem=table_recv.at[narrow],
             device_id=(w, n),
             device_id_type=MESH,
         ).start()
@@ -284,18 +291,25 @@
                 ]
         mine[f] = lined[...].reshape(blocks, rows, 128)
 
-    whole(table, table_sems.at[0], table_sems.at[1]).wait_recv()
-    to_scalar = pltpu.make_async_copy(table, table_smem, small_sem)
-    to_scalar.start()
-    to_scalar.wait()
-
-    def wanted(d):
-        return table_smem[d, 0, me]
-
-    def send_field(f):
+    def take_rows(plane):
+        rows_at = pl.ds(plane * wide_count, wide_count - 1 if plane is narrow else wide_count)
+        part = table.at[rows_at]
+        pltpu.make_async_remote_copy(
+            src_ref=part, dst_ref=part, send_sem=table_send, recv_sem=table_recv.at[plane],
+            device_id=(wide, narrow), device_id_type=MESH,
+        ).wait_recv()
+        rows_at = pl.ds(plane * wide_count, wide_count)
+        to_scalar = pltpu.make_async_copy(table.at[rows_at], table_smem.at[rows_at], small_sem)
+        to_scalar.start()
+        to_scalar.wait()
+
+    def wanted(w, n):
+        return table_smem[n * wide_count + w, 0, me]
+
+    def send_part(f):
         def send(w, n):
             d = w * narrow_count + n
-            stages[f][d] = mine[f, wanted(d)]
+            stages[f][d] = mine[f, wanted(w, n)]
             pltpu.make_async_remote_copy(
                 src_ref=stages[f].at[d],
                 dst_ref=lands[f].at[me],
@@ -305,10 +319,17 @@
                 device_id_type=MESH,
             ).start()
 
-        others(send)
+        return send
+
+    def send_field(f):
+        others(send_part(f))
         lands[f][me] = mine[f, my_own]
 
-    for f in range(AHEAD):
+    for plane in planes:
+        take_rows(plane)
+        to_plane(plane, send_part(0))
+    lands[0][me] = mine[0, my_own]
+    for f in range(1, AHEAD):
         send_field(f)
 
     for load in loads[FIELDS:]:
@@ -327,7 +348,7 @@
 
     def send_mean(w, n):
         d = w * narrow_count + n
-        mean_stage[d] = mean_mine[wanted(d)]
+        mean_stage[d] = mean_mine[wanted(w, n)]
         pltpu.make_async_remote_copy(
             src_ref=mean_stage.at[d],
             dst_ref=mean_land.at[me],
@@ -543,7 +564,7 @@
     over_rows(*wide_rows, DRIFT_TURNS, drift_rows)
     take_halo(FIELDS - 1)
 
-    whole(table, table_sems.at[0], table_sems.at[1]).wait_send()
+    whole(table, table_send, table_recv.at[0]).wait_send()
     whole(mean_land, mean_sems.at[0], mean_sems.at[1]).wait_send()
     for f in range(FIELDS):
         whole(lands[f], data_send.at[f], data_recv.at[f]).wait_send()
@@ -606,7 +627,8 @@
             pltpu.VMEM((FIELDS, 4, 8, nz), f32),
             pltpu.VMEM((FIELDS, 4, 8, nz), f32),
             dma((FIELDS + 3,)),
-            dma((2,)),
+            dma(()),
+            dma((narrow_count,)),
             dma((FIELDS,)),
             dma((FIELDS,)),
             dma((2,)),

time: 93 us -> 92 us (0.989)
  Pallas kernels: 92.2 us -> 91.2 us
    pallas_call x1, Pallas kernels: 89.6 us -> 88.7 us  [migrate(): pl.pallas_call(functools.partial(migrate_kernel, wide_count=wide_count, n...]
where the time goes in v7:
time: 92 us; the launch traced here: 91.8 us
  Pallas kernels  91.2 us (99%)
    pallas_call x1, Pallas kernels, migrate(): pl.pallas_call(functools.partial(migrate_kernel, wide_count=wide_count, n...  88.7 us
    pallas_call x1, Pallas kernels, relax_all(): pl.pallas_call(relax_kernel, out_shape=(jax.ShapeDtypeStruct((3, nx, ny,...  2.54 us

profile of v7, /device:TPU:1, one launch (start us, length us, event | category | flops | bytes accessed | tf_op | source)
XLA Modules:
  0.0 91.8 jit_solution(11800242970042098242)
XLA Ops:
  0.6 88.7 %shard_map.111 = (f32[4,888,128]{2,1,0:T(8,128)S(1)}, f32[4,888,128]{2,1,0:T(8,128)S(1)}, f32[6,888,128]{2,1,0:T(8,128)S(1)}, f32[3,888,128]{2,1,0:T(8,128)S(1)}...) custom-call(s32[16]{0:T(128)} %places_ref.1, f32[3,16,4096]{2,1,0:T(8,128)} %bitcast.3, f32[16,4096]{1,0:T(8,128)} %stress_ref.1, ...), custom_call_target="tpu_custom_call" | custom-call | tf_op jit(solution)/shard_map/pallas_call | solution.py:592
  89.3 2.5 %shard_map.112 = (f32[3,16,32,128]{3,2,1,0:T(8,128)}, f32[16,32,128]{2,1,0:T(8,128)}, f32[16,32,128]{2,1,0:T(8,128)}, f32[8,4,8,32]{3,2,1,0:T(8,128)}) custom-call(f32[4,888,128]{2,1,0:T(8,128)S(1)} %get-tuple-element.10.pad_ref, f32[4,888,128]{2,1,0:T(8,128)S(1)} %get-tuple-element.11.part_ref, f32[6,888,128]{2,1,0:T(8,128)S(1)} %get-tuple-element.12.side_ref, ...), custom_call_target="tpu_custom_call" | custom-call | tf_op jit(solution)/shard_map/pallas_call | solution.py:696

commit v8 on v7

--- a/solution.py
+++ b/solution.py
@@ -267,9 +267,6 @@
 
     others(send_row)
 
-    for ref in (pad_ref, eta, warm, edge_in, corner_in, corner_out):
-        ref[...] = jnp.zeros(ref.shape, jnp.float32)
-
     def whole(ref, send_sem, recv_sem):
         part = ref.at[pl.ds(0, count - 1)]
         return pltpu.make_async_remote_copy(
@@ -282,7 +279,7 @@
         )
 
     rows = BS * BS * BS // 128
-    for f in range(FIELDS):
+    def lay_out(f):
         loads[f].wait()
         for g in range(blocks // 8):
             for j in range(rows):
@@ -290,6 +287,8 @@
                     f, g * 8 : g * 8 + 8, j * 128 : j * 128 + 128
                 ]
         mine[f] = lined[...].reshape(blocks, rows, 128)
+
+    lay_out(0)
 
     def take_rows(plane):
         rows_at = pl.ds(plane * wide_count, wide_count - 1 if plane is narrow else wide_count)
@@ -322,15 +321,19 @@
         return send
 
     def send_field(f):
-        others(send_part(f))
+        others(send_part(f), farthest_first)
         lands[f][me] = mine[f, my_own]
 
     for plane in planes:
         take_rows(plane)
         to_plane(plane, send_part(0))
     lands[0][me] = mine[0, my_own]
-    for f in range(1, AHEAD):
-        send_field(f)
+    for ref in (pad_ref, eta, warm, edge_in, corner_in, corner_out):
+        ref[...] = jnp.zeros(ref.shape, jnp.float32)
+    for f in range(1, FIELDS):
+        lay_out(f)
+        if f < AHEAD:
+            send_field(f)
 
     for load in loads[FIELDS:]:
         load.wait()
@@ -418,7 +421,7 @@
         return found
 
     def each_message(g, act):
-        for way in ways:
+        for way in ways[4:] + ways[:4]:
             group = [m for m in messages(g) if m[0] == way]
 
             @pl.when(exists(way))
@@ -554,7 +557,9 @@
                     write_rows(f, pl.ds(row_of(x, y * BS), BS), part[x])
         if f == 1:
             viscosity()
-        send_halo(f)
+            send_halo(0)
+        if f > 0:
+            send_halo(f)
         if f == 3:
             take_halo(0)
             take_halo(1)

time: 92 us -> 91.5 us (level)
  no operation moved by 1% of the time
where the time goes in v8:
time: 91.5 us; the launch traced here: 91.3 us
  Pallas kernels  90.7 us (99%)
    pallas_call x1, Pallas kernels, migrate(): pl.pallas_call(functools.partial(migrate_kernel, wide_count=wide_count, n...  88.1 us
    pallas_call x1, Pallas kernels, relax_all(): pl.pallas_call(relax_kernel, out_shape=(jax.ShapeDtypeStruct((3, nx, ny,...  2.54 us

profile of v8, /device:TPU:1, one launch (start us, length us, event | category | flops | bytes accessed | tf_op | source)
XLA Modules:
  0.0 91.3 jit_solution(17062998050299990135)
XLA Ops:
  0.6 88.1 %shard_map.111 = (f32[4,888,128]{2,1,0:T(8,128)S(1)}, f32[4,888,128]{2,1,0:T(8,128)S(1)}, f32[6,888,128]{2,1,0:T(8,128)S(1)}, f32[3,888,128]{2,1,0:T(8,128)S(1)}...) custom-call(s32[16]{0:T(128)} %places_ref.1, f32[3,16,4096]{2,1,0:T(8,128)} %bitcast.3, f32[16,4096]{1,0:T(8,128)} %stress_ref.1, ...), custom_call_target="tpu_custom_call" | custom-call | tf_op jit(solution)/shard_map/pallas_call | solution.py:597
  88.8 2.5 %shard_map.112 = (f32[3,16,32,128]{3,2,1,0:T(8,128)}, f32[16,32,128]{2,1,0:T(8,128)}, f32[16,32,128]{2,1,0:T(8,128)}, f32[8,4,8,32]{3,2,1,0:T(8,128)}) custom-call(f32[4,888,128]{2,1,0:T(8,128)S(1)} %get-tuple-element.10.pad_ref, f32[4,888,128]{2,1,0:T(8,128)S(1)} %get-tuple-element.11.part_ref, f32[6,888,128]{2,1,0:T(8,128)S(1)} %get-tuple-element.12.side_ref, ...), custom_call_target="tpu_custom_call" | custom-call | tf_op jit(solution)/shard_map/pallas_call | solution.py:701

commit v9 on v8

--- a/solution.py
+++ b/solution.py
@@ -286,7 +286,7 @@
                 lined[pl.ds(g * 8 * rows + j, 8, stride=rows), :] = raw[
                     f, g * 8 : g * 8 + 8, j * 128 : j * 128 + 128
                 ]
-        mine[f] = lined[...].reshape(blocks, rows, 128)
+        mine[f] = lined[: blocks * rows].reshape(blocks, rows, 128)
 
     lay_out(0)
 
@@ -370,7 +370,7 @@
     def grid_part(f, y):
         for z in range(LZ):
             held[pl.ds(z, rows, stride=LZ), :] = lands[f][source_of(y, z)]
-        return swap_groups(held[...].reshape(rows, LZ, 128)).reshape(BS, BS, 128)
+        return swap_groups(held[: rows * LZ].reshape(rows, LZ, 128)).reshape(BS, BS, 128)
 
     ways = ((-1, 0), (1, 0), (0, -1), (0, 1), (-1, -1), (-1, 1), (1, -1), (1, 1))
     low_side = {-1: (wide > 0, narrow > 0), 1: (wide < wide_count - 1, narrow < narrow_count - 1)}
@@ -567,15 +567,12 @@
     for f in range(2, FIELDS - 1):
         take_halo(f)
     over_rows(*wide_rows, DRIFT_TURNS, drift_rows)
-    take_halo(FIELDS - 1)
-
     whole(table, table_send, table_recv.at[0]).wait_send()
     whole(mean_land, mean_sems.at[0], mean_sems.at[1]).wait_send()
     for f in range(FIELDS):
         whole(lands[f], data_send.at[f], data_recv.at[f]).wait_send()
-    for f in range(FIELDS):
         each_message(f, wait_message(f, True))
-
+    take_halo(FIELDS - 1)
 
 def migrate(slots, flow, stress, heat, drag, attributes, holder, voxel):
     wide_count, narrow_count = lax.axis_size("wide"), lax.axis_size("narrow")
@@ -612,7 +609,7 @@
             pltpu.VMEM((count, 1, 128), jnp.int32),
             pltpu.SMEM((count, 1, 128), jnp.int32),
             pltpu.VMEM((FIELDS, blocks, rows * 128), f32),
-            pltpu.VMEM((blocks * rows, 128), f32),
+            pltpu.VMEM((blocks * rows + rows, 128), f32),
             pltpu.VMEM((FIELDS, blocks, rows, 128), f32),
             *per_field,
             *per_field,
@@ -622,8 +619,8 @@
             pltpu.VMEM((blocks, 4, 128), f32),
             pltpu.VMEM((count, 4, 128), f32),
             pltpu.VMEM((count, 4, 128), f32),
-            pltpu.VMEM((4 * LZ, 128), f32),
-            pltpu.VMEM((rows * LZ, 128), f32),
+            pltpu.VMEM((4 * LZ + LZ, 128), f32),
+            pltpu.VMEM((rows * LZ + LZ, 128), f32),
             pltpu.VMEM((nx, ny, nz), f32),
             pltpu.VMEM((pad_rows, nz), f32),
             pltpu.VMEM((pad_rows, nz), f32),

time: 91.5 us -> 91.4 us (level)
  no operation moved by 1% of the time
where the time goes in v9:
time: 91.4 us; the launch traced here: 91.2 us
  Pallas kernels  90.6 us (99%)
    pallas_call x1, Pallas kernels, migrate(): pl.pallas_call(functools.partial(migrate_kernel, wide_count=wide_count, n...  88 us
    pallas_call x1, Pallas kernels, relax_all(): pl.pallas_call(relax_kernel, out_shape=(jax.ShapeDtypeStruct((3, nx, ny,...  2.54 us

profile of v9, /device:TPU:1, one launch (start us, length us, event | category | flops | bytes accessed | tf_op | source)
XLA Modules:
  0.0 91.2 jit_solution(6903614698296971463)
XLA Ops:
  0.6 88.0 %shard_map.111 = (f32[4,888,128]{2,1,0:T(8,128)S(1)}, f32[4,888,128]{2,1,0:T(8,128)S(1)}, f32[6,888,128]{2,1,0:T(8,128)S(1)}, f32[3,888,128]{2,1,0:T(8,128)S(1)}...) custom-call(s32[16]{0:T(128)} %places_ref.1, f32[3,16,4096]{2,1,0:T(8,128)} %bitcast.3, f32[16,4096]{1,0:T(8,128)} %stress_ref.1, ...), custom_call_target="tpu_custom_call" | custom-call | tf_op jit(solution)/shard_map/pallas_call | solution.py:594
  88.7 2.5 %shard_map.112 = (f32[3,16,32,128]{3,2,1,0:T(8,128)}, f32[16,32,128]{2,1,0:T(8,128)}, f32[16,32,128]{2,1,0:T(8,128)}, f32[8,4,8,32]{3,2,1,0:T(8,128)}) custom-call(f32[4,888,128]{2,1,0:T(8,128)S(1)} %get-tuple-element.10.pad_ref, f32[4,888,128]{2,1,0:T(8,128)S(1)} %get-tuple-element.11.part_ref, f32[6,888,128]{2,1,0:T(8,128)S(1)} %get-tuple-element.12.side_ref, ...), custom_call_target="tpu_custom_call" | custom-call | tf_op jit(solution)/shard_map/pallas_call | solution.py:698

commit v10 on v9

--- a/solution.py
+++ b/solution.py
@@ -626,8 +626,8 @@
             pltpu.VMEM((pad_rows, nz), f32),
             pltpu.VMEM((FIELDS, 2, DEEP, nx, nz), f32),
             pltpu.VMEM((FIELDS, 2, DEEP, nx, nz), f32),
-            pltpu.VMEM((FIELDS, 4, 8, nz), f32),
-            pltpu.VMEM((FIELDS, 4, 8, nz), f32),
+            pltpu.VMEM((FIELDS, 4, 4, nz), f32),
+            pltpu.VMEM((FIELDS, 4, 4, nz), f32),
             dma((FIELDS + 3,)),
             dma(()),
             dma((narrow_count,)),

time: 91.4 us -> 91.2 us (level)
  no operation moved by 1% of the time
where the time goes in v10:
time: 91.2 us; the launch traced here: 91 us
  Pallas kernels  90.4 us (99%)
    pallas_call x1, Pallas kernels, migrate(): pl.pallas_call(functools.partial(migrate_kernel, wide_count=wide_count, n...  87.8 us
    pallas_call x1, Pallas kernels, relax_all(): pl.pallas_call(relax_kernel, out_shape=(jax.ShapeDtypeStruct((3, nx, ny,...  2.54 us

profile of v10, /device:TPU:1, one launch (start us, length us, event | category | flops | bytes accessed | tf_op | source)
XLA Modules:
  0.0 91.0 jit_solution(744146565378917363)
XLA Ops:
  0.6 87.8 %shard_map.111 = (f32[4,888,128]{2,1,0:T(8,128)S(1)}, f32[4,888,128]{2,1,0:T(8,128)S(1)}, f32[6,888,128]{2,1,0:T(8,128)S(1)}, f32[3,888,128]{2,1,0:T(8,128)S(1)}...) custom-call(s32[16]{0:T(128)} %places_ref.1, f32[3,16,4096]{2,1,0:T(8,128)} %bitcast.3, f32[16,4096]{1,0:T(8,128)} %stress_ref.1, ...), custom_call_target="tpu_custom_call" | custom-call | tf_op jit(solution)/shard_map/pallas_call | solution.py:594
  88.5 2.5 %shard_map.112 = (f32[3,16,32,128]{3,2,1,0:T(8,128)}, f32[16,32,128]{2,1,0:T(8,128)}, f32[16,32,128]{2,1,0:T(8,128)}, f32[8,4,8,32]{3,2,1,0:T(8,128)}) custom-call(f32[4,888,128]{2,1,0:T(8,128)S(1)} %get-tuple-element.10.pad_ref, f32[4,888,128]{2,1,0:T(8,128)S(1)} %get-tuple-element.11.part_ref, f32[6,888,128]{2,1,0:T(8,128)S(1)} %get-tuple-element.12.side_ref, ...), custom_call_target="tpu_custom_call" | custom-call | tf_op jit(solution)/shard_map/pallas_call | solution.py:698

commit v11 on v10

--- a/solution.py
+++ b/solution.py
@@ -675,7 +675,7 @@
     over_rows(PITCH, (slabs - 1) * PITCH, TURNS, finish_first)
     over_rows(2 * PITCH, (slabs - 2) * PITCH, TURNS, second)
 
-    parts = 4
+    parts = 8
     thick = nx // parts
     for part in range(parts):
         for x in range(part * thick, (part + 1) * thick):
@@ -709,7 +709,7 @@
             pltpu.VMEM(pad.shape, jnp.float32),
             pltpu.VMEM(pad.shape, jnp.float32),
             pltpu.VMEM((4, nx, ny, nz), jnp.float32),
-            pltpu.SemaphoreType.DMA((10,)),
+            pltpu.SemaphoreType.DMA((18,)),
         ],
         compiler_params=pltpu.CompilerParams(vmem_limit_bytes=16 * 1024 * 1024),
     )(pad, part, side, rest, heat, means)

time: 91.2 us -> 91.3 us (level)
  no operation moved by 1% of the time
where the time goes in v11:
time: 91.3 us; the launch traced here: 91 us
  Pallas kernels  90.4 us (99%)
    pallas_call x1, Pallas kernels, migrate(): pl.pallas_call(functools.partial(migrate_kernel, wide_count=wide_count, n...  87.8 us
    pallas_call x1, Pallas kernels, relax_all(): pl.pallas_call(relax_kernel, out_shape=(jax.ShapeDtypeStruct((3, nx, ny,...  2.57 us

profile of v11, /device:TPU:1, one launch (start us, length us, event | category | flops | bytes accessed | tf_op | source)
XLA Modules:
  0.0 91.0 jit_solution(4988502834022245212)
XLA Ops:
  0.6 87.8 %shard_map.111 = (f32[4,888,128]{2,1,0:T(8,128)S(1)}, f32[4,888,128]{2,1,0:T(8,128)S(1)}, f32[6,888,128]{2,1,0:T(8,128)S(1)}, f32[3,888,128]{2,1,0:T(8,128)S(1)}...) custom-call(s32[16]{0:T(128)} %places_ref.1, f32[3,16,4096]{2,1,0:T(8,128)} %bitcast.3, f32[16,4096]{1,0:T(8,128)} %stress_ref.1, ...), custom_call_target="tpu_custom_call" | custom-call | tf_op jit(solution)/shard_map/pallas_call | solution.py:594
  88.5 2.6 %shard_map.112 = (f32[3,16,32,128]{3,2,1,0:T(8,128)}, f32[16,32,128]{2,1,0:T(8,128)}, f32[16,32,128]{2,1,0:T(8,128)}, f32[8,4,8,32]{3,2,1,0:T(8,128)}) custom-call(f32[4,888,128]{2,1,0:T(8,128)S(1)} %get-tuple-element.10.pad_ref, f32[4,888,128]{2,1,0:T(8,128)S(1)} %get-tuple-element.11.part_ref, f32[6,888,128]{2,1,0:T(8,128)S(1)} %get-tuple-element.12.side_ref, ...), custom_call_target="tpu_custom_call" | custom-call | tf_op jit(solution)/shard_map/pallas_call | solution.py:698
